TPU v7x, 32 devices: a whole 2x2x4 slice. The times are simulated.
32 devices in a mesh: subj: 4 (over y, x), slab: 8 (over z, core).
Axes of the slice: x: 2, y: 2, z: 4, core: 2. Of those that a mesh axis runs over, the one named last changes fastest.
Arguments:
- subjects: float32 [8, 64, 448, 128], P('subj', 'slab'), may hold values from -8 to 8
- templates: float32 [4, 64, 448, 128], P(None, 'slab', 'subj'), may hold values from -6 to 6
- labels: int32 [8], replicated, may hold values from 0 to 3, as said below
- group_live_counts: int32 [4], replicated, may hold values from 1 to 2, as said below
Outputs:
- new_templates: float32 [4, 64, 448, 128], P(None, 'slab', 'subj')
Inputs may be any that keep to these rules, and one draw needn't show every extreme that they name: `labels`: slot j belongs to group j // 2; slot 0 of group g has label g mod 4. The live slots of group g are its first group_live_counts[g] slots; the other slots hold volumes of no subject; some group has all 2 slots live.
All inputs are finite; a program needn't handle non-finite values.
Results may differ from a plain program's by a relative error of at most 0.00002.
Values sent between devices are 32-bit elements; how exact they have to be, the bound alone decides.
A program may use at most 192 MiB of HBM per device.

v0:
```python
import jax
import jax.numpy as jnp
from jax import lax
from jax.sharding import PartitionSpec as P

RADIUS = 4


epsilon = 1e-05
step_size = 0.5


def extended(block, sides, width):
    for axis, dim in sides:
        count = lax.axis_size(axis)
        forward = [(i, i + 1) for i in range(count - 1)]
        backward = [(target, source) for source, target in forward]
        low = lax.ppermute(
            lax.slice_in_dim(block, block.shape[dim] - width, None, axis=dim), axis, forward
        )
        high = lax.ppermute(lax.slice_in_dim(block, 0, width, axis=dim), axis, backward)
        block = jnp.concatenate([low, block, high], axis=dim)
    return block


def window_sum(volume, which_axis, extent):
    running = lax.slice_in_dim(volume, 0, extent, axis=which_axis)
    for offset in range(1, 2 * RADIUS + 1):
        running = running + lax.slice_in_dim(volume, offset, offset + extent, axis=which_axis)
    return running


def padded_sum(volume, which_axis):
    widths = [(0, 0)] * volume.ndim
    widths[which_axis] = (RADIUS, RADIUS)
    return window_sum(jnp.pad(volume, widths), which_axis, volume.shape[which_axis])


def plane_box(volume, leading):
    return padded_sum(padded_sum(volume, leading), leading + 1)


def similarity_gradient(subject_ext, template_ext, slab_depth, rim):
    window = float((2 * RADIUS + 1) ** 3)
    row_count = subject_ext.shape[0] - 2 * RADIUS
    channels = jnp.stack(
        [
            subject_ext,
            template_ext,
            subject_ext * subject_ext,
            template_ext * template_ext,
            subject_ext * template_ext,
        ]
    )
    local_sums = plane_box(window_sum(channels, 1, row_count), 2)
    subject_sum = local_sums[0]
    template_sum = local_sums[1]
    covariance = local_sums[4] - subject_sum * template_sum / window
    subject_variance = local_sums[2] - subject_sum * subject_sum / window
    template_variance = local_sums[3] - template_sum * template_sum / window
    denominator = subject_variance * template_variance + epsilon
    cross_weight = 2.0 * covariance / denominator
    spread_weight = -covariance * covariance * subject_variance / (denominator * denominator)
    mean_weight = -(cross_weight * subject_sum + 2.0 * spread_weight * template_sum) / window
    stacked = jnp.stack([mean_weight, cross_weight, spread_weight])
    stacked = extended(stacked, (("slab", 1),), RADIUS)
    filtered = plane_box(window_sum(stacked, 1, slab_depth), 2)
    centre_subject = subject_ext[rim : rim + slab_depth]
    centre_template = template_ext[rim : rim + slab_depth]
    return filtered[0] + filtered[1] * centre_subject + 2.0 * filtered[2] * centre_template


def per_device(subjects, templates, labels, group_live_counts):
    rim = RADIUS
    group_index = lax.axis_index("subj")
    slot_total = subjects.shape[0]
    slab_depth = subjects.shape[1]
    clusters = templates.shape[0]
    group_total = group_live_counts.shape[0]
    slot_positions = jnp.arange(labels.shape[0], dtype=jnp.int32)
    group_ids = jnp.arange(group_total, dtype=jnp.int32)
    slot_live_counts = jnp.sum(
        jnp.where(
            (slot_positions // slot_total)[:, None] == group_ids[None, :],
            group_live_counts[None, :],
            0,
        ),
        axis=1,
    )
    live_mask = (slot_positions % slot_total < slot_live_counts).astype(jnp.float32)
    cluster_membership = (labels[:, None] == jnp.arange(clusters, dtype=jnp.int32)[None, :]).astype(
        jnp.float32
    ) * live_mask[:, None]
    members = jnp.sum(cluster_membership, axis=0)
    rimmed = extended(templates, (("slab", 1),), rim)
    template_ext = lax.all_gather(rimmed, "subj", axis=2, tiled=True)
    subject_ext = extended(subjects, (("slab", 1),), rim)
    own_labels = lax.dynamic_slice_in_dim(labels, group_index * slot_total, slot_total)
    own_load = jnp.sum(jnp.where(group_ids == group_index, group_live_counts, 0))

    def accumulate(slot_number, cluster_totals):
        cluster_label = own_labels[slot_number]
        live_weight = (slot_number < own_load).astype(jnp.float32)
        subject = lax.dynamic_index_in_dim(subject_ext, slot_number, 0, keepdims=False)
        template = lax.dynamic_index_in_dim(template_ext, cluster_label, 0, keepdims=False)
        template_gradient = similarity_gradient(subject, template, slab_depth, rim)
        current = lax.dynamic_index_in_dim(cluster_totals, cluster_label, 0, keepdims=False)
        return lax.dynamic_update_index_in_dim(
            cluster_totals, current + live_weight * template_gradient, cluster_label, 0
        )

    empty = jnp.zeros((clusters, slab_depth, subjects.shape[2], subjects.shape[3]), jnp.float32)
    cluster_totals = lax.fori_loop(0, slot_total, accumulate, empty)
    summed = lax.psum_scatter(cluster_totals, "subj", scatter_dimension=2, tiled=True)
    return templates + step_size * summed / members[:, None, None, None]


def solution(mesh):
    in_specs = (P("subj", "slab", None, None), P(None, "slab", "subj", None), P(), P())
    out_specs = P(None, "slab", "subj", None)
    return jax.shard_map(
        per_device, mesh=mesh, in_specs=in_specs, out_specs=out_specs, check_vma=False
    )
```

profile of v0, /device:TPU:1, one launch (start us, length us, event | category | flops | bytes accessed | tf_op | source)
XLA Modules:
  0.0 693.6 jit_solution(7764220668136805117)
XLA Ops:
  8.1 4.6 collective-permute-start.4
  14.7 8.4 %collective-permute-done.4 = f32[4,4,112,128]{3,2,1,0:T(8,128)S(1)} collective-permute-done((f32[4,4,112,128]{3,2,1,0:T(8,128)S(1)}, f32[4,4,112,128]{3,2,1,0:T(8,128)S(1)}, u32[]{:S(2)}, u32[]{:S(2)}) %collective-permute-start.4) | collective-permute-done | bytes 917536 | tf_op jit(solution)/shard_map/ppermute | solution.py:18
  40.6 17.2 %collective-permute-done.2 = f32[2,4,448,128]{3,2,1,0:T(8,128)S(1)} collective-permute-done((f32[2,4,448,128]{3,2,1,0:T(8,128)}, f32[2,4,448,128]{3,2,1,0:T(8,128)S(1)}, u32[]{:S(2)}, u32[]{:S(2)}) %collective-permute-start.2) | collective-permute-done | bytes 1835040 | tf_op jit(solution)/shard_map/ppermute | solution.py:18
  57.8 4.7 collective-permute-done.3
  62.5 5.1 pad_maximum_fusion.2
  67.6 103.4 %all-gather.2.cloned.1.call-done = f32[4,16,448,128]{3,2,1,0:T(8,128)} async-done(((f32[4,16,112,128]{3,2,1,0:T(8,128)}), f32[4,16,448,128]{3,2,1,0:T(8,128)}) %all-gather.2.cloned.1.call-update) | async-done | bytes 14680080 | tf_op jit(solution)/shard_map/all_gather | solution.py:96
  174.8 431.3 %while.15 = (s32[]{:T(128)}, f32[4,8,448,128]{3,2,1,0:T(8,128)}, s32[2]{0:T(128)S(1)}, s32[]{:T(128)}, f32[2,16,448,128]{3,2,1,0:T(8,128)}, /*index=5*/f32[4,16,...) while((s32[]{:T(128)}, f32[4,8,448,128]{3,2,1,0:T(8,128)}, s32[2]{0:T(128)S(1)}, s32[]{:T(128)}, ...), condition=%wide.region_2.3_spmd, body=%wide.region_1.2_spmd.sunk | while | flops 122945536 | bytes 389022016 | solution.py:113
  181.6 4.4 dynamic-slice_dynamic-update-slice_fusion.5
  193.7 4.4 multiply_dynamic-update-slice_fusion.8
  198.1 27.4 %slice_add_fusion.21 = f32[5,8,448,128]{3,2,1,0:T(8,128)S(1)} fusion(f32[5,16,448,128]{3,2,1,0:T(8,128)} %multiply_dynamic-update-slice_fusion.8), kind=kLoop, calls=%fused_computation.24.clone.1 | loop fusion | flops 18350080 | bytes 91750400 | tf_op jit(solution)/shard_map/while/body/eval_jaxpr/add | solution.py:29
  225.5 8.6 %slice_add_fusion.22 = f32[5,8,448,128]{3,2,1,0:T(8,128)} fusion(f32[5,8,448,128]{3,2,1,0:T(8,128)S(1)} %slice_add_fusion.21), kind=kLoop, calls=%fused_computation.32.clone.1 | loop fusion | flops 18350080 | bytes 18350080 | tf_op jit(solution)/shard_map/while/body/eval_jaxpr/add | solution.py:29
  234.1 33.2 %fusion.39 = f32[5,8,448,128]{3,2,1,0:T(8,128)S(1)} fusion(f32[5,8,448,128]{3,2,1,0:T(8,128)} %slice_add_fusion.22), kind=kLoop, calls=%fused_computation.23.clone.1 | loop fusion | flops 18350080 | bytes 18350080 | tf_op jit(solution)/shard_map/while/body/eval_jaxpr/add | solution.py:29
  280.1 27.5 %collective-permute-done = f32[3,4,448,128]{3,2,1,0:T(8,128)} collective-permute-done((f32[3,4,448,128]{3,2,1,0:T(8,128)}, f32[3,4,448,128]{3,2,1,0:T(8,128)}, u32[]{:S(2)}, u32[]{:S(2)}) %collective-permute-start) | collective-permute-done | bytes 2752544 | tf_op jit(solution)/shard_map/while/body/eval_jaxpr/ppermute | solution.py:18
  307.6 4.4 collective-permute-done.1
  312.0 9.3 %maximum_maximum_fusion.2 = (f32[3,12,448,128]{3,2,1,0:T(8,128)}, f32[3,12,448,128]{3,2,1,0:T(8,128)}) fusion(f32[1,8,448,128]{3,2,1,0:T(8,128)} %copy-done.1, f32[1,8,448,128]{3,2,1,0:T(8,128)} %copy-done, f32[1,8,448,128]{3,2,1,0:T(8,128)S(1)} %get-tuple-element.229, f32[3,4,448,128]{3,2,1,0:T(8,128)} %collective-permute-done, ...), kind=kLoop, calls=%fused_computation.38.clone.1 | loop fusion | flops 12386304 | bytes 27525120 | tf_op jit(solution)/shard_map/while/body/eval_jaxpr/concatenate | solution.py:22
  321.3 19.3 %slice_add_fusion.23 = f32[3,8,448,128]{3,2,1,0:T(8,128)} fusion(f32[3,12,448,128]{3,2,1,0:T(8,128)} %get-tuple-element.232, f32[3,12,448,128]{3,2,1,0:T(8,128)} %get-tuple-element.233, f32[1,8,448,128]{3,2,1,0:T(8,128)} %copy-done.1, f32[1,8,448,128]{3,2,1,0:T(8,128)} %copy-done, f32[1,8,448,128]{3,2,1,0:T(8,128)S(1)} %get-tuple-element.229), kind=kLoop, calls=%fused_computation.48.clone.1 | loop fusion | flops 13762560 | bytes 55050240 | tf_op jit(solution)/shard_map/while/body/eval_jaxpr/add | solution.py:29
  340.6 20.4 %slice_add_fusion.24 = f32[3,8,448,128]{3,2,1,0:T(8,128)} fusion(f32[3,8,448,128]{3,2,1,0:T(8,128)} %slice_add_fusion.23), kind=kLoop, calls=%fused_computation.57.clone.1 | loop fusion | flops 11010048 | bytes 11010048 | tf_op jit(solution)/shard_map/while/body/eval_jaxpr/add | solution.py:29
  361.0 24.2 %fusion.41 = f32[3,8,448,128]{3,2,1,0:T(8,128)} fusion(f32[3,8,448,128]{3,2,1,0:T(8,128)} %slice_add_fusion.24), kind=kLoop, calls=%fused_computation.47.clone.1 | loop fusion | flops 11010048 | bytes 11010048 | tf_op jit(solution)/shard_map/while/body/eval_jaxpr/add | solution.py:29
  385.2 6.1 fusion.42
  398.1 4.4 dynamic-slice_dynamic-update-slice_fusion.5
  410.2 4.4 multiply_dynamic-update-slice_fusion.8
  414.6 27.4 %slice_add_fusion.21 = f32[5,8,448,128]{3,2,1,0:T(8,128)S(1)} fusion(f32[5,16,448,128]{3,2,1,0:T(8,128)} %multiply_dynamic-update-slice_fusion.8), kind=kLoop, calls=%fused_computation.24.clone.1 | loop fusion | flops 18350080 | bytes 91750400 | tf_op jit(solution)/shard_map/while/body/eval_jaxpr/add | solution.py:29
  442.0 8.6 %slice_add_fusion.22 = f32[5,8,448,128]{3,2,1,0:T(8,128)} fusion(f32[5,8,448,128]{3,2,1,0:T(8,128)S(1)} %slice_add_fusion.21), kind=kLoop, calls=%fused_computation.32.clone.1 | loop fusion | flops 18350080 | bytes 18350080 | tf_op jit(solution)/shard_map/while/body/eval_jaxpr/add | solution.py:29
  450.6 33.2 %fusion.39 = f32[5,8,448,128]{3,2,1,0:T(8,128)S(1)} fusion(f32[5,8,448,128]{3,2,1,0:T(8,128)} %slice_add_fusion.22), kind=kLoop, calls=%fused_computation.23.clone.1 | loop fusion | flops 18350080 | bytes 18350080 | tf_op jit(solution)/shard_map/while/body/eval_jaxpr/add | solution.py:29
  496.6 25.8 %collective-permute-done = f32[3,4,448,128]{3,2,1,0:T(8,128)} collective-permute-done((f32[3,4,448,128]{3,2,1,0:T(8,128)}, f32[3,4,448,128]{3,2,1,0:T(8,128)}, u32[]{:S(2)}, u32[]{:S(2)}) %collective-permute-start) | collective-permute-done | bytes 2752544 | tf_op jit(solution)/shard_map/while/body/eval_jaxpr/ppermute | solution.py:18
  522.3 4.4 collective-permute-done.1
  526.7 9.3 %maximum_maximum_fusion.2 = (f32[3,12,448,128]{3,2,1,0:T(8,128)}, f32[3,12,448,128]{3,2,1,0:T(8,128)}) fusion(f32[1,8,448,128]{3,2,1,0:T(8,128)} %copy-done.1, f32[1,8,448,128]{3,2,1,0:T(8,128)} %copy-done, f32[1,8,448,128]{3,2,1,0:T(8,128)S(1)} %get-tuple-element.229, f32[3,4,448,128]{3,2,1,0:T(8,128)} %collective-permute-done, ...), kind=kLoop, calls=%fused_computation.38.clone.1 | loop fusion | flops 12386304 | bytes 27525120 | tf_op jit(solution)/shard_map/while/body/eval_jaxpr/concatenate | solution.py:22
  536.0 19.3 %slice_add_fusion.23 = f32[3,8,448,128]{3,2,1,0:T(8,128)} fusion(f32[3,12,448,128]{3,2,1,0:T(8,128)} %get-tuple-element.232, f32[3,12,448,128]{3,2,1,0:T(8,128)} %get-tuple-element.233, f32[1,8,448,128]{3,2,1,0:T(8,128)} %copy-done.1, f32[1,8,448,128]{3,2,1,0:T(8,128)} %copy-done, f32[1,8,448,128]{3,2,1,0:T(8,128)S(1)} %get-tuple-element.229), kind=kLoop, calls=%fused_computation.48.clone.1 | loop fusion | flops 13762560 | bytes 55050240 | tf_op jit(solution)/shard_map/while/body/eval_jaxpr/add | solution.py:29
  555.4 20.4 %slice_add_fusion.24 = f32[3,8,448,128]{3,2,1,0:T(8,128)} fusion(f32[3,8,448,128]{3,2,1,0:T(8,128)} %slice_add_fusion.23), kind=kLoop, calls=%fused_computation.57.clone.1 | loop fusion | flops 11010048 | bytes 11010048 | tf_op jit(solution)/shard_map/while/body/eval_jaxpr/add | solution.py:29
  575.8 24.2 %fusion.41 = f32[3,8,448,128]{3,2,1,0:T(8,128)} fusion(f32[3,8,448,128]{3,2,1,0:T(8,128)} %slice_add_fusion.24), kind=kLoop, calls=%fused_computation.47.clone.1 | loop fusion | flops 11010048 | bytes 11010048 | tf_op jit(solution)/shard_map/while/body/eval_jaxpr/add | solution.py:29
  599.9 6.1 fusion.42
  607.0 76.8 %reduce-scatter.2.cloned.1.call-done = f32[4,8,112,128]{3,2,1,0:T(8,128)} async-done(((f32[4,8,448,128]{3,2,1,0:T(8,128)}), f32[4,8,112,128]{3,2,1,0:T(8,128)}) %reduce-scatter.2.cloned.1.call-update) | async-done | bytes 1835024 | tf_op jit(solution)/shard_map/reduce_scatter | solution.py:114
  (59 shorter events, 77.9 us)
Async XLA Ops:
  6.5 164.4 %all-gather.2.cloned.1.call-start = ((), (), s32[]{:S(2)}) async-start(), calls=%async_computation.1 | async-start | bytes 18350080 | tf_op jit(solution)/shard_map/all_gather | solution.py:96
  8.1 14.9 %collective-permute-start.4 = (f32[4,4,112,128]{3,2,1,0:T(8,128)S(1)}, f32[4,4,112,128]{3,2,1,0:T(8,128)S(1)}, u32[]{:S(2)}, u32[]{:S(2)}) collective-permute-start(f32[4,4,112,128]{3,2,1,0:T(8,128)S(1)} %get-tuple-element.181), channel_id=1, source_target_pairs={{0,1},{1,2},{2,3},{3,4},{4,5},{5,6},{6,7},{8,9},{9,10},{10,11},{11... | collective-permute-start | bytes 2752520 | tf_op jit(solution)/shard_map/ppermute | solution.py:18
  12.7 14.7 %collective-permute-start.5 = (f32[4,4,112,128]{3,2,1,0:T(8,128)S(1)}, f32[4,4,112,128]{3,2,1,0:T(8,128)S(1)}, u32[]{:S(2)}, u32[]{:S(2)}) collective-permute-start(f32[4,4,112,128]{3,2,1,0:T(8,128)S(1)} %get-tuple-element.182), channel_id=1, source_target_pairs={{1,0},{2,1},{3,2},{4,3},{5,4},{6,5},{7,6},{9,8},{10,9},{11,10},{12... | collective-permute-start | bytes 2752520 | tf_op jit(solution)/shard_map/ppermute | solution.py:21
  31.1 8.8 %copy-start.6 = (s32[8]{0:T(128)S(1)}, s32[8]{0:T(128)}, u32[]{:S(2)}) copy-start(s32[8]{0:T(128)} %param.8) | copy-start | bytes 100
  31.1 8.9 %copy-start.4 = (s32[4]{0:T(128)S(1)}, s32[4]{0:T(128)}, u32[]{:S(2)}) copy-start(s32[4]{0:T(128)} %param.9) | copy-start | bytes 52
  31.1 652.6 %reduce-scatter.2.cloned.1.call-start = ((), (), s32[]{:S(2)}) async-start(), calls=%async_computation.2 | async-start | bytes 9175040 | tf_op jit(solution)/shard_map/reduce_scatter | solution.py:114
  35.4 22.4 %collective-permute-start.2 = (f32[2,4,448,128]{3,2,1,0:T(8,128)}, f32[2,4,448,128]{3,2,1,0:T(8,128)S(1)}, u32[]{:S(2)}, u32[]{:S(2)}) collective-permute-start(f32[2,4,448,128]{3,2,1,0:T(8,128)} %get-tuple-element.179), channel_id=1, source_target_pairs={{0,1},{1,2},{2,3},{3,4},{4,5},{5,6},{6,7},{8,9},{9,10},{10,11},{11... | collective-permute-start | bytes 5505032 | tf_op jit(solution)/shard_map/ppermute | solution.py:18
  37.4 25.2 %collective-permute-start.3 = (f32[2,4,448,128]{3,2,1,0:T(8,128)}, f32[2,4,448,128]{3,2,1,0:T(8,128)}, u32[]{:S(2)}, u32[]{:S(2)}) collective-permute-start(f32[2,4,448,128]{3,2,1,0:T(8,128)} %get-tuple-element.180), channel_id=1, source_target_pairs={{1,0},{2,1},{3,2},{4,3},{5,4},{6,5},{7,6},{9,8},{10,9},{11,10},{12... | collective-permute-start | bytes 5505032 | tf_op jit(solution)/shard_map/ppermute | solution.py:21
  181.6 5.5 copy-start.2
  268.8 1.3 copy-start
  268.8 1.8 copy-start.1
  273.6 34.0 %collective-permute-start = (f32[3,4,448,128]{3,2,1,0:T(8,128)}, f32[3,4,448,128]{3,2,1,0:T(8,128)}, u32[]{:S(2)}, u32[]{:S(2)}) collective-permute-start(f32[3,4,448,128]{3,2,1,0:T(8,128)} %get-tuple-element.230), channel_id=1, source_target_pairs={{0,1},{1,2},{2,3},{3,4},{4,5},{5,6},{6,7},{8,9},{9,10},{10,11},{11... | collective-permute-start | bytes 8257544 | tf_op jit(solution)/shard_map/while/body/eval_jaxpr/ppermute | solution.py:18
  277.3 34.7 %collective-permute-start.1 = (f32[3,4,448,128]{3,2,1,0:T(8,128)}, f32[3,4,448,128]{3,2,1,0:T(8,128)}, u32[]{:S(2)}, u32[]{:S(2)}) collective-permute-start(f32[3,4,448,128]{3,2,1,0:T(8,128)} %get-tuple-element.231), channel_id=1, source_target_pairs={{1,0},{2,1},{3,2},{4,3},{5,4},{6,5},{7,6},{9,8},{10,9},{11,10},{12... | collective-permute-start | bytes 8257544 | tf_op jit(solution)/shard_map/while/body/eval_jaxpr/ppermute | solution.py:21
  398.1 5.5 copy-start.2
  485.3 1.3 copy-start
  485.3 1.8 copy-start.1
  490.1 32.2 %collective-permute-start = (f32[3,4,448,128]{3,2,1,0:T(8,128)}, f32[3,4,448,128]{3,2,1,0:T(8,128)}, u32[]{:S(2)}, u32[]{:S(2)}) collective-permute-start(f32[3,4,448,128]{3,2,1,0:T(8,128)} %get-tuple-element.230), channel_id=1, source_target_pairs={{0,1},{1,2},{2,3},{3,4},{4,5},{5,6},{6,7},{8,9},{9,10},{10,11},{11... | collective-permute-start | bytes 8257544 | tf_op jit(solution)/shard_map/while/body/eval_jaxpr/ppermute | solution.py:18
  492.0 34.7 %collective-permute-start.1 = (f32[3,4,448,128]{3,2,1,0:T(8,128)}, f32[3,4,448,128]{3,2,1,0:T(8,128)}, u32[]{:S(2)}, u32[]{:S(2)}) collective-permute-start(f32[3,4,448,128]{3,2,1,0:T(8,128)} %get-tuple-element.231), channel_id=1, source_target_pairs={{1,0},{2,1},{3,2},{4,3},{5,4},{6,5},{7,6},{9,8},{10,9},{11,10},{12... | collective-permute-start | bytes 8257544 | tf_op jit(solution)/shard_map/while/body/eval_jaxpr/ppermute | solution.py:21
  606.1 0.7 copy-start.5
  606.1 0.7 copy-start.7
  606.1 77.7 %copy-start.3 = (f32[4,8,112,128]{3,2,1,0:T(8,128)S(1)}, f32[4,8,112,128]{3,2,1,0:T(8,128)}, u32[]{:S(2)}) copy-start(f32[4,8,112,128]{3,2,1,0:T(8,128)} %param.7) | copy-start | bytes 5505028
Sparse Core Ops, SparseCore 0:
  31.2 139.6 all-gather.1
  606.2 77.4 reduce-scatter.1
where the time goes:
time: 695 us; the launch traced here: 694 us
  other arithmetic  336 us (48%)
  waiting for transfers between devices  277 us (40%)
  local copies, waits for them, and re-layouts  39.6 us (6%)
  starting transfers between devices  22.6 us (3%)
  between operations  13.5 us (2%)
    add x12, other arithmetic, window_sum(): running + lax.slice_in_dim(volume, offset, offset + extent, axis=which_axis)  266 us
    all_gather x1, waiting for transfers between devices, per_device(): template_ext = lax.all_gather(rimmed, 'subj', axis=2, tiled=True)  103 us
    ppermute x4, waiting for transfers between devices, extended(): lax.ppermute(lax.slice_in_dim(block, block.shape[dim] - width, None, axis...  78.8 us
    reduce_scatter x1, waiting for transfers between devices, per_device(): lax.psum_scatter(cluster_totals, 'subj', scatter_dimension=2, tiled=True)  76.8 us
    concatenate x4, other arithmetic, extended(): block = jnp.concatenate([low, block, high], axis=dim)  27.4 us
    while x16, local copies, waits for them, and re-layouts  22.1 us
    ppermute x4, waiting for transfers between devices, extended(): lax.ppermute(lax.slice_in_dim(block, 0, width, axis=dim), axis, backward)  17.9 us
  transfers between devices with their start and end apart: 10, of which 10 were waited for; matrix products, arithmetic and copies ran while one was open for 1% of the time, Pallas kernels for 0%

commit v1 on v0

v1 whole, which is shorter than its diff:
```python
import functools

import jax
import jax.numpy as jnp
from jax import lax
from jax.experimental import pallas as pl
from jax.experimental.pallas import tpu as pltpu
from jax.sharding import PartitionSpec as P

RADIUS = 4
WIDTH = 2 * RADIUS + 1
CELLS = float(WIDTH**3)

epsilon = 1e-05
step_size = 0.5


def halo(block, axis, dim, width):
    count = lax.axis_size(axis)
    forward = [(i, i + 1) for i in range(count - 1)]
    backward = [(target, source) for source, target in forward]
    size = block.shape[dim]
    low = lax.ppermute(lax.slice_in_dim(block, size - width, size, axis=dim), axis, forward)
    high = lax.ppermute(lax.slice_in_dim(block, 0, width, axis=dim), axis, backward)
    return low, high


def thirds(value):
    high = value.astype(jnp.bfloat16)
    rest = value - high.astype(jnp.float32)
    middle = rest.astype(jnp.bfloat16)
    low = (rest - middle.astype(jnp.float32)).astype(jnp.bfloat16)
    return [high, middle, low]


def plane_box(planes, band_x, band_y):
    count = len(planes)
    rows = band_x.shape[0]
    terms = [jnp.concatenate(thirds(plane), axis=0) for plane in planes]
    along_x = [jnp.dot(band_x, term, preferred_element_type=jnp.float32) for term in terms]
    stacked = jnp.concatenate([jnp.concatenate(thirds(v), axis=1) for v in along_x], axis=0)
    summed = jnp.dot(stacked, band_y, preferred_element_type=jnp.float32)
    return [summed[i * rows : (i + 1) * rows] for i in range(count)]


def kernel(
    labels, live, low, mid, high, templates, band_1, band_2, band_y, totals, whole, sums, boxes
):
    slot = pl.program_id(0)
    clusters, extended = templates.shape[0], templates.shape[1]
    depth = mid.shape[1]
    own = totals.shape[2]
    rim = 2 * RADIUS

    @pl.when(slot == 0)
    def _():
        totals[...] = jnp.zeros_like(totals)

        def prepare(step, carry):
            k, z = step // depth, step % depth
            first = templates[k, z]
            total, square = first, first * first
            for offset in range(1, WIDTH):
                layer = templates[k, z + offset]
                total, square = total + layer, square + layer * layer
            total, square = plane_box([total, square], band_1[...], band_y[...])
            sums[k, z, 0] = total
            sums[k, z, 1] = square - total * total * (1.0 / CELLS)
            return carry

        lax.fori_loop(0, clusters * depth, prepare, 0, unroll=2)

    @pl.when(live[slot] > 0)
    def _():
        label = labels[slot]
        whole[0:RADIUS] = low[0]
        whole[RADIUS : RADIUS + depth] = mid[0]
        whole[RADIUS + depth : extended] = high[0]

        def layer(z, carry):
            s, t = whole[z], templates[label, z]
            total, square, product = s, s * s, s * t
            for offset in range(1, WIDTH):
                s, t = whole[z + offset], templates[label, z + offset]
                total, square, product = total + s, square + s * s, product + s * t
            s_sum, s_square, cross = plane_box([total, square, product], band_1[...], band_y[...])
            t_sum, t_variance = sums[label, z, 0], sums[label, z, 1]
            covariance = cross - s_sum * t_sum * (1.0 / CELLS)
            s_variance = s_square - s_sum * s_sum * (1.0 / CELLS)
            ratio = covariance / (s_variance * t_variance + epsilon)
            p = 2.0 * ratio
            q_twice = -2.0 * ratio * ratio * s_variance
            a = -(p * s_sum + q_twice * t_sum) * (1.0 / CELLS)
            result = plane_box([a, p, q_twice], band_2[...], band_y[...])
            for channel in range(3):
                boxes[z, channel] = result[channel]
            return carry

        lax.fori_loop(0, depth, layer, 0, unroll=2)

        chunk = 16 if own % 16 == 0 else 8

        def add_up(index, carry):
            start = pl.multiple_of(index * chunk, chunk)
            rows = pl.ds(start, chunk)
            inner = pl.ds(pl.multiple_of(start + rim, 8), chunk)
            for order, shift in ((range(depth), 0), (reversed(range(depth)), extended - depth)):
                running = [None] * 3
                for z in order:
                    terms = [boxes[z, channel, rows] for channel in range(3)]
                    running = [
                        new if old is None else old + new for old, new in zip(running, terms)
                    ]
                    out = z + shift
                    totals[label, out, rows] += (
                        running[0]
                        + running[1] * whole[out, inner]
                        + running[2] * templates[label, out, inner]
                    )
            return carry

        lax.fori_loop(0, own // chunk, add_up, 0)


def per_device(subjects, templates, labels, group_live_counts):
    groups = lax.axis_size("subj")
    position = lax.axis_index("subj")
    group_slots, depth, length, breadth = subjects.shape
    clusters, _, own, _ = templates.shape
    slots = labels.shape[0]
    rim = 2 * RADIUS
    rows = -(-(own + 2 * rim) // 16) * 16
    extended = depth + 2 * RADIUS

    slot_ids = jnp.arange(slots, dtype=jnp.int32)
    live = (slot_ids % group_slots < jnp.repeat(group_live_counts, group_slots)).astype(jnp.int32)
    membership = (labels[:, None] == jnp.arange(clusters, dtype=jnp.int32)[None, :]) & (
        live[:, None] > 0
    )
    members = jnp.sum(membership.astype(jnp.float32), axis=0)

    padded = jnp.pad(subjects, ((0, 0), (0, 0), (rim, rows - own - rim), (0, 0)))
    parts = jnp.stack(
        [lax.slice_in_dim(padded, i * own, i * own + rows, axis=2) for i in range(groups)]
    )
    mine = lax.all_to_all(parts, "subj", 0, 0, tiled=True).reshape(slots, depth, rows, breadth)
    s_low, s_high = halo(mine, "slab", 1, RADIUS)

    t_low, t_high = halo(templates, "slab", 1, RADIUS)
    t_deep = jnp.concatenate([t_low, templates, t_high], axis=1)
    x_low, x_high = halo(t_deep, "subj", 2, rim)
    t_whole = jnp.concatenate([x_low, t_deep, x_high], axis=2)
    if rows > own + 2 * rim:
        t_whole = jnp.pad(t_whole, ((0, 0), (0, 0), (0, rows - own - 2 * rim), (0, 0)))

    def band(out, count, inside):
        i = lax.broadcasted_iota(jnp.int32, (out, rows), 0)
        j = lax.broadcasted_iota(jnp.int32, (out, rows), 1)
        kept = (j >= i) & (j - i < WIDTH) & (i < count) & inside(j)
        return jnp.concatenate([kept.astype(jnp.bfloat16)] * 3, axis=1)

    def in_grid(j):
        x = position * own + j - RADIUS
        return (x >= 0) & (x < length)

    band_1 = band(rows, own + rim, lambda j: j >= 0)
    band_2 = band(own, own, in_grid)
    i = lax.broadcasted_iota(jnp.int32, (breadth, breadth), 0)
    j = lax.broadcasted_iota(jnp.int32, (breadth, breadth), 1)
    band_y = jnp.concatenate([(jnp.abs(i - j) <= RADIUS).astype(jnp.bfloat16)] * 3, axis=0)

    def whole_block(array):
        return pl.BlockSpec(array.shape, lambda slot, *_: (0,) * array.ndim)

    def slot_block(array):
        return pl.BlockSpec((1,) + array.shape[1:], lambda slot, *_: (slot, 0, 0, 0))

    out_shape = jax.ShapeDtypeStruct((clusters, extended, own, breadth), jnp.float32)
    totals = pl.pallas_call(
        kernel,
        grid_spec=pltpu.PrefetchScalarGridSpec(
            num_scalar_prefetch=2,
            grid=(slots,),
            in_specs=[
                slot_block(s_low),
                slot_block(mine),
                slot_block(s_high),
                whole_block(t_whole),
                whole_block(band_1),
                whole_block(band_2),
                whole_block(band_y),
            ],
            out_specs=whole_block(out_shape),
            scratch_shapes=[
                pltpu.VMEM((extended, rows, breadth), jnp.float32),
                pltpu.VMEM((clusters, depth, 2, rows, breadth), jnp.float32),
                pltpu.VMEM((depth, 3, own, breadth), jnp.float32),
            ],
        ),
        out_shape=out_shape,
        compiler_params=pltpu.CompilerParams(vmem_limit_bytes=48 * 1024 * 1024),
    )(labels, live, s_low, mine, s_high, t_whole, band_1, band_2, band_y)

    count = lax.axis_size("slab")
    forward = [(i, i + 1) for i in range(count - 1)]
    backward = [(target, source) for source, target in forward]
    from_low = lax.ppermute(totals[:, depth + RADIUS :], "slab", forward)
    from_high = lax.ppermute(totals[:, :RADIUS], "slab", backward)
    summed = totals[:, RADIUS : RADIUS + depth]
    middle = ((0, 0), (0, depth - RADIUS), (0, 0), (0, 0))
    summed = summed + jnp.pad(from_low, middle)
    summed = summed + jnp.pad(from_high, (middle[0], middle[1][::-1]) + middle[2:])
    return templates + step_size * summed / members[:, None, None, None]


def solution(mesh):
    in_specs = (P("subj", "slab", None, None), P(None, "slab", "subj", None), P(), P())
    out_specs = P(None, "slab", "subj", None)
    return jax.shard_map(
        per_device, mesh=mesh, in_specs=in_specs, out_specs=out_specs, check_vma=False
    )
```

time: 695 us -> 167 us (0.24)
  other arithmetic: 336 us -> 10.3 us
  waiting for transfers between devices: 277 us -> 64 us
  Pallas kernels: 0 us -> 50.3 us
  local copies, waits for them, and re-layouts: 39.6 us -> 13 us
  between operations: 13.5 us -> 0.25 us
    add x12 -> x0, other arithmetic: 266 us -> none  [window_sum(): running + lax.slice_in_dim(volume, offset, offset + extent, axis=which_axis)]
    all_gather x1 -> x0, waiting for transfers between devices: 103 us -> none  [per_device(): template_ext = lax.all_gather(rimmed, 'subj', axis=2, tiled=True)]
    reduce_scatter x1 -> x0, waiting for transfers between devices: 76.8 us -> none  [per_device(): lax.psum_scatter(cluster_totals, 'subj', scatter_dimension=2, tiled=True)]
    ppermute x8, waiting for transfers between devices: 96.7 us -> 23.9 us  [the longest x1 8.27 us: per_device(): from_low = lax.ppermute(totals[:, depth + RADIUS:], 'slab', forward)]
    pallas_call x0 -> x1, Pallas kernels: none -> 50.3 us  [per_device(): pl.pallas_call(kernel, grid_spec=pltpu.PrefetchScalarGridSpec(num_scalar_...]
    all_to_all x0 -> x1, waiting for transfers between devices: none -> 40.1 us  [per_device(): lax.all_to_all(parts, 'subj', 0, 0, tiled=True)]
    concatenate x4, other arithmetic: 27.4 us -> 4.62 us  [the longest x1 4.57 us: per_device(): t_whole = jnp.concatenate([x_low, t_deep, x_high], axis=2)]
    while x16 -> x0, local copies, waits for them, and re-layouts: 22.1 us -> none
  transfers between devices with their start and end apart: 10 -> 9, of which waited for: 10 -> 5; matrix products, arithmetic and copies ran while one was open for 1% -> 8% of each run, Pallas kernels for 0% -> 0%
where the time goes in v1:
time: 167 us; the launch traced here: 166 us
  waiting for transfers between devices  64 us (38%)
  Pallas kernels  50.3 us (30%)
  starting transfers between devices  28.5 us (17%)
  local copies, waits for them, and re-layouts  13 us (8%)
  other arithmetic  10.3 us (6%)
    pallas_call x1, Pallas kernels, per_device(): pl.pallas_call(kernel, grid_spec=pltpu.PrefetchScalarGridSpec(num_scalar_...  50.3 us
    all_to_all x1, waiting for transfers between devices, per_device(): lax.all_to_all(parts, 'subj', 0, 0, tiled=True)  40.1 us
    ppermute x3, starting transfers between devices, halo(): lax.ppermute(lax.slice_in_dim(block, size - width, size, axis=dim), axis,...  10.7 us
    ppermute x1, waiting for transfers between devices, per_device(): from_low = lax.ppermute(totals[:, depth + RADIUS:], 'slab', forward)  8.27 us
    ppermute x3, waiting for transfers between devices, halo(): lax.ppermute(lax.slice_in_dim(block, 0, width, axis=dim), axis, backward)  7.61 us
    ppermute x3, starting transfers between devices, halo(): lax.ppermute(lax.slice_in_dim(block, 0, width, axis=dim), axis, backward)  6.67 us
    slice x2, local copies, waits for them, and re-layouts, halo(): lax.slice_in_dim(block, 0, width, axis=dim)  5.89 us
    all_to_all x1, starting transfers between devices, per_device(): lax.all_to_all(parts, 'subj', 0, 0, tiled=True)  4.98 us
  transfers between devices with their start and end apart: 9, of which 5 were waited for; matrix products, arithmetic and copies ran while one was open for 8% of the time, Pallas kernels for 0%

profile of v1, /device:TPU:1, one launch (start us, length us, event | category | flops | bytes accessed | tf_op | source)
XLA Modules:
  0.0 166.4 jit_solution(16628039582893393186)
XLA Ops:
  0.0 2.6 %fusion.4 = (f32[1,2,8,128,128]{4,3,2,1,0:T(8,128)S(1)}, f32[1,2,8,128,128]{4,3,2,1,0:T(8,128)S(1)}, f32[1,2,8,128,128]{4,3,2,1,0:T(8,128)S(1)}, f32[1,2,8,128,128]{4,3,2,1,0:T(8,128)S(1)}) fusion(f32[2,8,448,128]{3,2,1,0:T(8,128)} %param.4), kind=kLoop, calls=%fused_computation.9 | loop fusion | bytes 9961472 | tf_op jit(solution)/shard_map/stack | solution.py:143
  2.6 2.3 %pad_maximum_fusion = f32[4,2,8,128,128]{4,3,2,1,0:T(8,128)} fusion(f32[1,2,8,128,128]{4,3,2,1,0:T(8,128)S(1)} %get-tuple-element.14, f32[1,2,8,128,128]{4,3,2,1,0:T(8,128)S(1)} %get-tuple-element.15, f32[1,2,8,128,128]{4,3,2,1,0:T(8,128)S(1)} %get-tuple-element.16, f32[1,2,8,128,128]{4,3,2,1,0:T(8,128)S(1)} %get-tuple-element.13), kind=kLoop, calls=%fused_computation | loop fusion | flops 3145728 | bytes 8388608 | tf_op jit(solution)/shard_map/stack | solution.py:143
  4.9 5.0 %all-to-all-start = ((f32[4,2,8,128,128]{4,3,2,1,0:T(8,128)}), f32[4,2,8,128,128]{4,3,2,1,0:T(8,128)}, u32[]{:S(2)}, u32[]{:S(2)}) async-start(f32[4,2,8,128,128]{4,3,2,1,0:T(8,128)} %pad_maximum_fusion), calls=%async_computation | async-start | bytes 8388608 | tf_op jit(solution)/shard_map/all_to_all | solution.py:146
  9.8 1.1 fusion.17
  10.9 2.3 %collective-permute-start.3 = (f32[4,4,112,128]{3,2,1,0:T(8,128)S(1)}, f32[4,4,112,128]{3,2,1,0:T(8,128)}, u32[]{:S(2)}, u32[]{:S(2)}) collective-permute-start(f32[4,4,112,128]{3,2,1,0:T(8,128)S(1)} %get-tuple-element.17), channel_id=1, source_target_pairs={{1,0},{2,1},{3,2},{4,3},{5,4},{6,5},{7,6},{9,8},{10,9},{11,10},{12... | collective-permute-start | bytes 2752520 | tf_op jit(solution)/shard_map/ppermute | solution.py:24
  13.2 4.2 %collective-permute-start.2 = (f32[4,4,112,128]{3,2,1,0:T(8,128)}, f32[4,4,112,128]{3,2,1,0:T(8,128)}, u32[]{:S(2)}, u32[]{:S(2)}) collective-permute-start(f32[4,4,112,128]{3,2,1,0:T(8,128)} %get-tuple-element.18), channel_id=1, source_target_pairs={{0,1},{1,2},{2,3},{3,4},{4,5},{5,6},{6,7},{8,9},{9,10},{10,11},{11... | collective-permute-start | bytes 2752520 | tf_op jit(solution)/shard_map/ppermute | solution.py:23
  17.5 40.1 %all-to-all-done = f32[4,2,8,128,128]{4,3,2,1,0:T(8,128)} async-done(((f32[4,2,8,128,128]{4,3,2,1,0:T(8,128)}), f32[4,2,8,128,128]{4,3,2,1,0:T(8,128)}, u32[]{:S(2)}, u32[]{:S(2)}) %all-to-all-start) | async-done | bytes 4194336 | tf_op jit(solution)/shard_map/all_to_all | solution.py:146
  57.6 4.8 %fusion.14 = (f32[8,4,128,128]{3,2,1,0:T(8,128)}, f32[8,4,128,128]{3,2,1,0:T(8,128)}) fusion(f32[8,8,128,128]{3,2,1,0:T(8,128)} %bitcast.4.mid), kind=kLoop, calls=%fused_computation.40 | loop fusion | bytes 8388608 | tf_op jit(solution)/shard_map/slice | solution.py:24
  62.4 3.1 %collective-permute-start.1 = (f32[8,4,128,128]{3,2,1,0:T(8,128)}, f32[8,4,128,128]{3,2,1,0:T(8,128)S(1)}, u32[]{:S(2)}, u32[]{:S(2)}) collective-permute-start(f32[8,4,128,128]{3,2,1,0:T(8,128)} %get-tuple-element.7), channel_id=1, source_target_pairs={{1,0},{2,1},{3,2},{4,3},{5,4},{6,5},{7,6},{9,8},{10,9},{11,10},{12... | collective-permute-start | bytes 6291464 | tf_op jit(solution)/shard_map/ppermute | solution.py:24
  65.5 3.3 %collective-permute-start = (f32[8,4,128,128]{3,2,1,0:T(8,128)}, f32[8,4,128,128]{3,2,1,0:T(8,128)}, u32[]{:S(2)}, u32[]{:S(2)}) collective-permute-start(f32[8,4,128,128]{3,2,1,0:T(8,128)} %get-tuple-element.8), channel_id=1, source_target_pairs={{0,1},{1,2},{2,3},{3,4},{4,5},{5,6},{6,7},{8,9},{9,10},{10,11},{11... | collective-permute-start | bytes 6291464 | tf_op jit(solution)/shard_map/ppermute | solution.py:23
  68.9 0.1 fusion.8
  69.0 0.1 fusion.12
  69.1 0.0 collective-permute-done.2
  69.1 1.2 constant_dynamic-update-slice_fusion.2
  70.4 0.0 copy-start.5
  70.4 0.1 constant_dynamic-update-slice_fusion.1
  70.6 1.2 constant_dynamic-update-slice_fusion
  71.9 3.1 %collective-permute-start.4 = (f32[4,16,8,128]{3,2,1,0:T(8,128)S(1)}, f32[4,16,8,128]{3,2,1,0:T(8,128)S(1)}, u32[]{:S(2)}, u32[]{:S(2)}) collective-permute-start(f32[4,16,8,128]{3,2,1,0:T(8,128)S(1)} %get-tuple-element.11), channel_id=1, source_target_pairs={{0,8},{8,16},{16,24},{1,9},{9,17},{17,25},{2,10},{10,18},{18,26},{... | collective-permute-start | bytes 786440 | tf_op jit(solution)/shard_map/ppermute | solution.py:23
  74.9 1.3 collective-permute-start.5
  76.3 0.1 broadcast_in_dim.2
  76.3 0.1 reshape.25
  76.4 3.6 %collective-permute-done.4 = f32[4,16,8,128]{3,2,1,0:T(8,128)S(1)} collective-permute-done((f32[4,16,8,128]{3,2,1,0:T(8,128)S(1)}, f32[4,16,8,128]{3,2,1,0:T(8,128)S(1)}, u32[]{:S(2)}, u32[]{:S(2)}) %collective-permute-start.4) | collective-permute-done | bytes 262176 | tf_op jit(solution)/shard_map/ppermute | solution.py:23
  80.0 7.6 %collective-permute-done.5 = f32[4,16,8,128]{3,2,1,0:T(8,128)S(1)} collective-permute-done((f32[4,16,8,128]{3,2,1,0:T(8,128)S(1)}, f32[4,16,8,128]{3,2,1,0:T(8,128)S(1)}, u32[]{:S(2)}, u32[]{:S(2)}) %collective-permute-start.5) | collective-permute-done | bytes 262176 | tf_op jit(solution)/shard_map/ppermute | solution.py:24
  87.6 4.6 %pad_maximum_fusion.1.templates = f32[4,16,128,128]{3,2,1,0:T(8,128)} fusion(f32[4,16,8,128]{3,2,1,0:T(8,128)S(1)} %collective-permute-done.5, f32[4,16,112,128]{3,2,1,0:T(8,128)} %copy-done.4, f32[4,16,8,128]{3,2,1,0:T(8,128)S(1)} %collective-permute-done.4), kind=kLoop, calls=%fused_computation.1 | loop fusion | flops 2097152 | bytes 8388608 | tf_op jit(solution)/shard_map/concatenate | solution.py:152
  92.2 50.3 %shard_map.46 = f32[4,16,112,128]{3,2,1,0:T(8,128)} custom-call(s32[8]{0:T(128)S(1)} %copy-done, s32[8]{0:T(128)S(1)} %get-tuple-element.6.live, f32[8,4,128,128]{3,2,1,0:T(8,128)} %collective-permute-done.low, f32[8,8,128,128]{3,2,1,0:T(8,128)} %bitcast.4.mid, f32[8,4,128,128]{3,2,1,0:T(8,128)S(1)} %collective-permute-done.1.high, ...), custom_call_target="tpu_custom_call" | custom-call | tf_op jit(solution)/shard_map/pallas_call | solution.py:179
  142.6 1.7 %fusion.15 = (f32[4,4,112,128]{3,2,1,0:T(8,128)S(1)}, f32[4,4,112,128]{3,2,1,0:T(8,128)S(1)}) fusion(f32[4,16,112,128]{3,2,1,0:T(8,128)} %shard_map.46), kind=kLoop, calls=%fused_computation.41 | loop fusion | bytes 3670016 | tf_op jit(solution)/shard_map/slice | solution.py:207
  144.3 4.3 %collective-permute-start.6 = (f32[4,4,112,128]{3,2,1,0:T(8,128)S(1)}, f32[4,4,112,128]{3,2,1,0:T(8,128)S(1)}, u32[]{:S(2)}, u32[]{:S(2)}) collective-permute-start(f32[4,4,112,128]{3,2,1,0:T(8,128)S(1)} %get-tuple-element.9), channel_id=1, source_target_pairs={{0,1},{1,2},{2,3},{3,4},{4,5},{5,6},{6,7},{8,9},{9,10},{10,11},{11... | collective-permute-start | bytes 2752520 | tf_op jit(solution)/shard_map/ppermute | solution.py:207
  148.6 1.9 %collective-permute-start.7 = (f32[4,4,112,128]{3,2,1,0:T(8,128)S(1)}, f32[4,4,112,128]{3,2,1,0:T(8,128)S(1)}, u32[]{:S(2)}, u32[]{:S(2)}) collective-permute-start(f32[4,4,112,128]{3,2,1,0:T(8,128)S(1)} %get-tuple-element.10), channel_id=1, source_target_pairs={{1,0},{2,1},{3,2},{4,3},{5,4},{6,5},{7,6},{9,8},{10,9},{11,10},{12... | collective-permute-start | bytes 2752520 | tf_op jit(solution)/shard_map/ppermute | solution.py:208
  150.5 0.1 convert_reduce_fusion
  150.7 8.3 %collective-permute-done.6 = f32[4,4,112,128]{3,2,1,0:T(8,128)S(1)} collective-permute-done((f32[4,4,112,128]{3,2,1,0:T(8,128)S(1)}, f32[4,4,112,128]{3,2,1,0:T(8,128)S(1)}, u32[]{:S(2)}, u32[]{:S(2)}) %collective-permute-start.6) | collective-permute-done | bytes 917536 | tf_op jit(solution)/shard_map/ppermute | solution.py:207
  158.9 4.4 %collective-permute-done.7 = f32[4,4,112,128]{3,2,1,0:T(8,128)S(1)} collective-permute-done((f32[4,4,112,128]{3,2,1,0:T(8,128)S(1)}, f32[4,4,112,128]{3,2,1,0:T(8,128)S(1)}, u32[]{:S(2)}, u32[]{:S(2)}) %collective-permute-start.7) | collective-permute-done | bytes 917536 | tf_op jit(solution)/shard_map/ppermute | solution.py:208
  163.3 3.1 %fusion.3 = f32[4,8,112,128]{3,2,1,0:T(8,128)} fusion(f32[4,8,112,128]{3,2,1,0:T(8,128)S(1)} %copy-done.3, f32[4,16,112,128]{3,2,1,0:T(8,128)} %shard_map.46, f32[4,4,112,128]{3,2,1,0:T(8,128)S(1)} %collective-permute-done.7, f32[4,4,112,128]{3,2,1,0:T(8,128)S(1)} %collective-permute-done.6, f32[4]{0:T(128)S(1)} %convert_reduce_fusion), kind=kLoop, calls=%fused_computation.8 | loop fusion | flops 2293760 | bytes 7340048 | tf_op jit(solution)/shard_map/add | solution.py:213
  (23 shorter events, 0.2 us)
Async XLA Ops:
  4.9 5.0 %copy-start.1 = (f32[4,8,112,128]{3,2,1,0:T(8,128)S(1)}, f32[4,8,112,128]{3,2,1,0:T(8,128)}, u32[]{:S(2)}) copy-start(f32[4,8,112,128]{3,2,1,0:T(8,128)} %param.5) | copy-start | bytes 5505028
  4.9 52.7 %all-to-all-start = ((f32[4,2,8,128,128]{4,3,2,1,0:T(8,128)}), f32[4,2,8,128,128]{4,3,2,1,0:T(8,128)}, u32[]{:S(2)}, u32[]{:S(2)}) async-start(f32[4,2,8,128,128]{4,3,2,1,0:T(8,128)} %pad_maximum_fusion), calls=%async_computation | async-start | bytes 8388608 | tf_op jit(solution)/shard_map/all_to_all | solution.py:146
  10.9 59.6 %collective-permute-start.3 = (f32[4,4,112,128]{3,2,1,0:T(8,128)S(1)}, f32[4,4,112,128]{3,2,1,0:T(8,128)}, u32[]{:S(2)}, u32[]{:S(2)}) collective-permute-start(f32[4,4,112,128]{3,2,1,0:T(8,128)S(1)} %get-tuple-element.17), channel_id=1, source_target_pairs={{1,0},{2,1},{3,2},{4,3},{5,4},{6,5},{7,6},{9,8},{10,9},{11,10},{12... | collective-permute-start | bytes 2752520 | tf_op jit(solution)/shard_map/ppermute | solution.py:24
  13.2 56.0 %collective-permute-start.2 = (f32[4,4,112,128]{3,2,1,0:T(8,128)}, f32[4,4,112,128]{3,2,1,0:T(8,128)}, u32[]{:S(2)}, u32[]{:S(2)}) collective-permute-start(f32[4,4,112,128]{3,2,1,0:T(8,128)} %get-tuple-element.18), channel_id=1, source_target_pairs={{0,1},{1,2},{2,3},{3,4},{4,5},{5,6},{6,7},{8,9},{9,10},{10,11},{11... | collective-permute-start | bytes 2752520 | tf_op jit(solution)/shard_map/ppermute | solution.py:23
  57.6 12.8 %copy-start.2 = (f32[4,8,112,128]{3,2,1,0:T(8,128)S(1)}, f32[4,8,112,128]{3,2,1,0:T(8,128)}, u32[]{:S(2)}) copy-start(f32[4,8,112,128]{3,2,1,0:T(8,128)} %param.5) | copy-start | bytes 5505028
  62.4 29.8 %collective-permute-start.1 = (f32[8,4,128,128]{3,2,1,0:T(8,128)}, f32[8,4,128,128]{3,2,1,0:T(8,128)S(1)}, u32[]{:S(2)}, u32[]{:S(2)}) collective-permute-start(f32[8,4,128,128]{3,2,1,0:T(8,128)} %get-tuple-element.7), channel_id=1, source_target_pairs={{1,0},{2,1},{3,2},{4,3},{5,4},{6,5},{7,6},{9,8},{10,9},{11,10},{12... | collective-permute-start | bytes 6291464 | tf_op jit(solution)/shard_map/ppermute | solution.py:24
  65.5 26.7 %collective-permute-start = (f32[8,4,128,128]{3,2,1,0:T(8,128)}, f32[8,4,128,128]{3,2,1,0:T(8,128)}, u32[]{:S(2)}, u32[]{:S(2)}) collective-permute-start(f32[8,4,128,128]{3,2,1,0:T(8,128)} %get-tuple-element.8), channel_id=1, source_target_pairs={{0,1},{1,2},{2,3},{3,4},{4,5},{5,6},{6,7},{8,9},{9,10},{10,11},{11... | collective-permute-start | bytes 6291464 | tf_op jit(solution)/shard_map/ppermute | solution.py:23
  70.4 5.9 %copy-start.5 = (s32[4]{0:T(128)S(1)}, s32[4]{0:T(128)}, u32[]{:S(2)}) copy-start(s32[4]{0:T(128)} %param.7) | copy-start | bytes 52
  71.8 3.1 %copy-start.4 = (f32[4,16,112,128]{3,2,1,0:T(8,128)}, f32[4,16,112,128]{3,2,1,0:T(8,128)S(1)}, u32[]{:S(2)}) copy-start(f32[4,16,112,128]{3,2,1,0:T(8,128)S(1)} %constant_dynamic-update-slice_fusion) | copy-start | bytes 11010052
  71.9 8.2 %collective-permute-start.4 = (f32[4,16,8,128]{3,2,1,0:T(8,128)S(1)}, f32[4,16,8,128]{3,2,1,0:T(8,128)S(1)}, u32[]{:S(2)}, u32[]{:S(2)}) collective-permute-start(f32[4,16,8,128]{3,2,1,0:T(8,128)S(1)} %get-tuple-element.11), channel_id=1, source_target_pairs={{0,8},{8,16},{16,24},{1,9},{9,17},{17,25},{2,10},{10,18},{18,26},{... | collective-permute-start | bytes 786440 | tf_op jit(solution)/shard_map/ppermute | solution.py:23
  74.9 12.7 %collective-permute-start.5 = (f32[4,16,8,128]{3,2,1,0:T(8,128)S(1)}, f32[4,16,8,128]{3,2,1,0:T(8,128)S(1)}, u32[]{:S(2)}, u32[]{:S(2)}) collective-permute-start(f32[4,16,8,128]{3,2,1,0:T(8,128)S(1)} %get-tuple-element.12), channel_id=1, source_target_pairs={{8,0},{16,8},{24,16},{9,1},{17,9},{25,17},{10,2},{18,10},{26,18},{... | collective-permute-start | bytes 786440 | tf_op jit(solution)/shard_map/ppermute | solution.py:24
  76.4 15.8 %copy-start = (s32[8]{0:T(128)S(1)}, s32[8]{0:T(128)}, u32[]{:S(2)}) copy-start(s32[8]{0:T(128)} %labels.1) | copy-start | bytes 100
  142.6 20.8 %copy-start.3 = (f32[4,8,112,128]{3,2,1,0:T(8,128)S(1)}, f32[4,8,112,128]{3,2,1,0:T(8,128)}, u32[]{:S(2)}) copy-start(f32[4,8,112,128]{3,2,1,0:T(8,128)} %param.5) | copy-start | bytes 5505028
  144.3 14.6 %collective-permute-start.6 = (f32[4,4,112,128]{3,2,1,0:T(8,128)S(1)}, f32[4,4,112,128]{3,2,1,0:T(8,128)S(1)}, u32[]{:S(2)}, u32[]{:S(2)}) collective-permute-start(f32[4,4,112,128]{3,2,1,0:T(8,128)S(1)} %get-tuple-element.9), channel_id=1, source_target_pairs={{0,1},{1,2},{2,3},{3,4},{4,5},{5,6},{6,7},{8,9},{9,10},{10,11},{11... | collective-permute-start | bytes 2752520 | tf_op jit(solution)/shard_map/ppermute | solution.py:207
  148.6 14.7 %collective-permute-start.7 = (f32[4,4,112,128]{3,2,1,0:T(8,128)S(1)}, f32[4,4,112,128]{3,2,1,0:T(8,128)S(1)}, u32[]{:S(2)}, u32[]{:S(2)}) collective-permute-start(f32[4,4,112,128]{3,2,1,0:T(8,128)S(1)} %get-tuple-element.10), channel_id=1, source_target_pairs={{1,0},{2,1},{3,2},{4,3},{5,4},{6,5},{7,6},{9,8},{10,9},{11,10},{12... | collective-permute-start | bytes 2752520 | tf_op jit(solution)/shard_map/ppermute | solution.py:208

commit v2 on v1

--- a/solution.py
+++ b/solution.py
@@ -43,32 +43,40 @@
     return [summed[i * rows : (i + 1) * rows] for i in range(count)]
 
 
-def kernel(
-    labels, live, low, mid, high, templates, band_1, band_2, band_y, totals, whole, sums, boxes
-):
+def template_kernel(templates, band_1, band_y, sums):
+    def prepare(z, carry):
+        first = templates[0, z]
+        total, square = first, first * first
+        for offset in range(1, WIDTH):
+            layer = templates[0, z + offset]
+            total, square = total + layer, square + layer * layer
+        total, square = plane_box([total, square], band_1[...], band_y[...])
+        sums[0, z, 0] = total
+        sums[0, z, 1] = square - total * total * (1.0 / CELLS)
+        return carry
+
+    lax.fori_loop(0, sums.shape[1], prepare, 0, unroll=2)
+
+
+def kernel(labels, live, low, mid, high, templates, sums, band_1, band_2, band_y, *rest):
+    given, (*outputs, whole, boxes) = rest[:-5], rest[-5:]
     slot = pl.program_id(0)
-    clusters, extended = templates.shape[0], templates.shape[1]
+    extended = templates.shape[1]
     depth = mid.shape[1]
-    own = totals.shape[2]
+    own = outputs[0].shape[2]
     rim = 2 * RADIUS
+
+    def place(out):
+        if out < RADIUS:
+            return outputs[0], out
+        if out < RADIUS + depth:
+            return outputs[1], out - RADIUS
+        return outputs[2], out - RADIUS - depth
 
     @pl.when(slot == 0)
     def _():
-        totals[...] = jnp.zeros_like(totals)
-
-        def prepare(step, carry):
-            k, z = step // depth, step % depth
-            first = templates[k, z]
-            total, square = first, first * first
-            for offset in range(1, WIDTH):
-                layer = templates[k, z + offset]
-                total, square = total + layer, square + layer * layer
-            total, square = plane_box([total, square], band_1[...], band_y[...])
-            sums[k, z, 0] = total
-            sums[k, z, 1] = square - total * total * (1.0 / CELLS)
-            return carry
-
-        lax.fori_loop(0, clusters * depth, prepare, 0, unroll=2)
+        for index, output in enumerate(outputs):
+            output[...] = given[index][...] if given else jnp.zeros_like(output)
 
     @pl.when(live[slot] > 0)
     def _():
@@ -112,7 +120,8 @@
                         new if old is None else old + new for old, new in zip(running, terms)
                     ]
                     out = z + shift
-                    totals[label, out, rows] += (
+                    output, position = place(out)
+                    output[label, position, rows] += (
                         running[0]
                         + running[1] * whole[out, inner]
                         + running[2] * templates[label, out, inner]
@@ -139,13 +148,6 @@
     )
     members = jnp.sum(membership.astype(jnp.float32), axis=0)
 
-    padded = jnp.pad(subjects, ((0, 0), (0, 0), (rim, rows - own - rim), (0, 0)))
-    parts = jnp.stack(
-        [lax.slice_in_dim(padded, i * own, i * own + rows, axis=2) for i in range(groups)]
-    )
-    mine = lax.all_to_all(parts, "subj", 0, 0, tiled=True).reshape(slots, depth, rows, breadth)
-    s_low, s_high = halo(mine, "slab", 1, RADIUS)
-
     t_low, t_high = halo(templates, "slab", 1, RADIUS)
     t_deep = jnp.concatenate([t_low, templates, t_high], axis=1)
     x_low, x_high = halo(t_deep, "subj", 2, rim)
@@ -170,43 +172,94 @@
     band_y = jnp.concatenate([(jnp.abs(i - j) <= RADIUS).astype(jnp.bfloat16)] * 3, axis=0)
 
     def whole_block(array):
-        return pl.BlockSpec(array.shape, lambda slot, *_: (0,) * array.ndim)
-
-    def slot_block(array):
-        return pl.BlockSpec((1,) + array.shape[1:], lambda slot, *_: (slot, 0, 0, 0))
-
-    out_shape = jax.ShapeDtypeStruct((clusters, extended, own, breadth), jnp.float32)
-    totals = pl.pallas_call(
-        kernel,
-        grid_spec=pltpu.PrefetchScalarGridSpec(
-            num_scalar_prefetch=2,
-            grid=(slots,),
-            in_specs=[
-                slot_block(s_low),
-                slot_block(mine),
-                slot_block(s_high),
-                whole_block(t_whole),
-                whole_block(band_1),
-                whole_block(band_2),
-                whole_block(band_y),
-            ],
-            out_specs=whole_block(out_shape),
-            scratch_shapes=[
-                pltpu.VMEM((extended, rows, breadth), jnp.float32),
-                pltpu.VMEM((clusters, depth, 2, rows, breadth), jnp.float32),
-                pltpu.VMEM((depth, 3, own, breadth), jnp.float32),
-            ],
+        return pl.BlockSpec(array.shape, lambda step, *_: (0,) * array.ndim)
+
+    def step_block(array, first=0):
+        return pl.BlockSpec(
+            (1,) + array.shape[1:], lambda step, *_: (step + first,) + (0,) * (array.ndim - 1)
+        )
+
+    sums_shape = jax.ShapeDtypeStruct((clusters, depth, 2, rows, breadth), jnp.float32)
+    sums = pl.pallas_call(
+        template_kernel,
+        grid=(clusters,),
+        in_specs=[step_block(t_whole), whole_block(band_1), whole_block(band_y)],
+        out_specs=step_block(sums_shape),
+        out_shape=sums_shape,
+        compiler_params=pltpu.CompilerParams(vmem_limit_bytes=24 * 1024 * 1024),
+        cost_estimate=pl.CostEstimate(
+            flops=10**10, bytes_accessed=2 * t_whole.size * 4, transcendentals=0
         ),
-        out_shape=out_shape,
-        compiler_params=pltpu.CompilerParams(vmem_limit_bytes=48 * 1024 * 1024),
-    )(labels, live, s_low, mine, s_high, t_whole, band_1, band_2, band_y)
+    )(t_whole, band_1, band_y)
+
+    def redistributed(slot):
+        wide = jnp.pad(subjects[slot], ((0, 0), (rim, rows - own - rim), (0, 0)))
+        parts = jnp.stack(
+            [lax.slice_in_dim(wide, i * own, i * own + rows, axis=1) for i in range(groups)]
+        )
+        return parts
+
+    out_shape = [
+        jax.ShapeDtypeStruct((clusters, layers, own, breadth), jnp.float32)
+        for layers in (RADIUS, depth, RADIUS)
+    ]
+    parts = [redistributed(slot) for slot in range(group_slots)]
+    arrived = []
+    for slot in range(group_slots):
+        send = parts[slot]
+        if arrived:
+            send, arrived[-1] = lax.optimization_barrier((send, arrived[-1]))
+        arrived.append(lax.all_to_all(send, "subj", 0, 0, tiled=True))
+    calls = []
+    for slot in range(group_slots):
+        split = slot + 1 < group_slots and groups % 2 == 0
+        size = groups // 2 if split else groups
+        calls += [(slot, first, size) for first in range(0, groups, size)]
+    totals = []
+    for slot, first, size in calls:
+        if first == 0:
+            mine = arrived[slot]
+            s_low, s_high = halo(mine, "slab", 1, RADIUS)
+        elif slot + 1 < group_slots:
+            arrived[slot + 1], *totals = lax.optimization_barrier((arrived[slot + 1], *totals))
+        totals = pl.pallas_call(
+            kernel,
+            grid_spec=pltpu.PrefetchScalarGridSpec(
+                num_scalar_prefetch=2,
+                grid=(size,),
+                in_specs=[step_block(v, first) for v in (s_low, mine, s_high)]
+                + [whole_block(v) for v in (t_whole, sums, band_1, band_2, band_y, *totals)],
+                out_specs=[whole_block(v) for v in out_shape],
+                scratch_shapes=[
+                    pltpu.VMEM((extended, rows, breadth), jnp.float32),
+                    pltpu.VMEM((depth, 3, own, breadth), jnp.float32),
+                ],
+            ),
+            out_shape=out_shape,
+            compiler_params=pltpu.CompilerParams(vmem_limit_bytes=48 * 1024 * 1024),
+            cost_estimate=pl.CostEstimate(
+                flops=2 * 10**9 * size, bytes_accessed=0, transcendentals=0
+            ),
+        )(
+            labels[slot::group_slots][first : first + size],
+            live[slot::group_slots][first : first + size],
+            s_low,
+            mine,
+            s_high,
+            t_whole,
+            sums,
+            band_1,
+            band_2,
+            band_y,
+            *totals,
+        )
 
     count = lax.axis_size("slab")
     forward = [(i, i + 1) for i in range(count - 1)]
     backward = [(target, source) for source, target in forward]
-    from_low = lax.ppermute(totals[:, depth + RADIUS :], "slab", forward)
-    from_high = lax.ppermute(totals[:, :RADIUS], "slab", backward)
-    summed = totals[:, RADIUS : RADIUS + depth]
+    from_low = lax.ppermute(totals[2], "slab", forward)
+    from_high = lax.ppermute(totals[0], "slab", backward)
+    summed = totals[1]
     middle = ((0, 0), (0, depth - RADIUS), (0, 0), (0, 0))
     summed = summed + jnp.pad(from_low, middle)
     summed = summed + jnp.pad(from_high, (middle[0], middle[1][::-1]) + middle[2:])

time: 167 us -> 151 us (0.904); the launches traced: 166 us -> 153 us
  waiting for transfers between devices: 64 us -> 23 us
  Pallas kernels: 50.3 us -> 67.4 us
  starting transfers between devices: 28.5 us -> 34.4 us
  local copies, waits for them, and re-layouts: 13 us -> 18.7 us
    all_to_all x1 -> x2, waiting for transfers between devices: 40.1 us -> 0.01 us  [per_device(): arrived.append(lax.all_to_all(send, 'subj', 0, 0, tiled=True))]
    pallas_call x0 -> x1, Pallas kernels: none -> 9.42 us  [per_device(): pl.pallas_call(template_kernel, grid=(clusters,), in_specs=[step_block(t_...]
    pallas_call x1 -> x3, Pallas kernels: 50.3 us -> 58 us  [per_device(): pl.pallas_call(kernel, grid_spec=pltpu.PrefetchScalarGridSpec(num_scalar_...]
    unnamed x14 -> x26, local copies, waits for them, and re-layouts: 1.4 us -> 6.85 us
    concatenate x1, other arithmetic: 4.57 us -> 0.5 us  [per_device(): t_whole = jnp.concatenate([x_low, t_deep, x_high], axis=2)]
    all_to_all x1 -> x2, starting transfers between devices: 4.98 us -> 8.72 us  [per_device(): arrived.append(lax.all_to_all(send, 'subj', 0, 0, tiled=True))]
    squeeze x0 -> x1, local copies, waits for them, and re-layouts: none -> 2.31 us  [redistributed(): wide = jnp.pad(subjects[slot], ((0, 0), (rim, rows - own - rim), (0, 0)))]
    another operation x1 -> x2, other arithmetic: 2.26 us -> 4.53 us  [redistributed(): jnp.stack([lax.slice_in_dim(wide, i * own, i * own + rows, axis=1) for i...]
  transfers between devices with their start and end apart: 9 -> 12, of which waited for: 5 -> 6; matrix products, arithmetic and copies ran while one was open for 8% -> 7% of each run, Pallas kernels for 0% -> 31%
where the time goes in v2:
time: 151 us; the launch traced here: 153 us
  Pallas kernels  67.4 us (45%)
  starting transfers between devices  34.4 us (23%)
  waiting for transfers between devices  23 us (15%)
  local copies, waits for them, and re-layouts  18.7 us (12%)
  other arithmetic  8.64 us (6%)
    pallas_call x3, Pallas kernels, per_device(): pl.pallas_call(kernel, grid_spec=pltpu.PrefetchScalarGridSpec(num_scalar_...  58 us
    ppermute x4, starting transfers between devices, halo(): lax.ppermute(lax.slice_in_dim(block, size - width, size, axis=dim), axis,...  12.1 us
    pallas_call x1, Pallas kernels, per_device(): pl.pallas_call(template_kernel, grid=(clusters,), in_specs=[step_block(t_...  9.42 us
    all_to_all x2, starting transfers between devices, per_device(): arrived.append(lax.all_to_all(send, 'subj', 0, 0, tiled=True))  8.72 us
    ppermute x4, starting transfers between devices, halo(): lax.ppermute(lax.slice_in_dim(block, 0, width, axis=dim), axis, backward)  8.72 us
    ppermute x1, waiting for transfers between devices, per_device(): from_low = lax.ppermute(totals[2], 'slab', forward)  8.27 us
    unnamed x26, local copies, waits for them, and re-layouts  6.85 us
    slice x3, local copies, waits for them, and re-layouts, halo(): lax.slice_in_dim(block, 0, width, axis=dim)  6.15 us
  transfers between devices with their start and end apart: 12, of which 6 were waited for; matrix products, arithmetic and copies ran while one was open for 7% of the time, Pallas kernels for 31%

profile of v2, /device:TPU:1, one launch (start us, length us, event | category | flops | bytes accessed | tf_op | source)
XLA Modules:
  0.0 152.5 jit_solution(7583575876612886146)
XLA Ops:
  0.0 2.3 %slice_bitcast_fusion = (f32[8,448,128]{2,1,0:T(8,128)S(1)}, f32[8,448,128]{2,1,0:T(8,128)S(1)}) fusion(f32[2,8,448,128]{3,2,1,0:T(8,128)} %param.4), kind=kLoop, calls=%fused_computation.4 | loop fusion | bytes 7340032 | tf_op jit(solution)/shard_map/squeeze | solution.py:196
  2.3 1.5 %fusion = (f32[1,8,128,128]{3,2,1,0:T(8,128)S(1)}, f32[1,8,128,128]{3,2,1,0:T(8,128)S(1)}, f32[1,8,128,128]{3,2,1,0:T(8,128)}, f32[1,8,128,128]{3,2,1,0:T(8,128)...) fusion(f32[8,448,128]{2,1,0:T(8,128)S(1)} %get-tuple-element.40, ...), kind=kLoop, calls=%fused_computation.10 | loop fusion | bytes 9961472 | tf_op jit(solution)/shard_map/stack | solution.py:197
  3.9 1.5 pad_maximum_fusion.2
  5.4 4.3 %all-to-all-start = ((f32[4,8,128,128]{3,2,1,0:T(8,128)}), f32[4,8,128,128]{3,2,1,0:T(8,128)S(1)}, u32[]{:S(2)}, u32[]{:S(2)}) async-start(f32[4,8,128,128]{3,2,1,0:T(8,128)} %pad_maximum_fusion.2), calls=%async_computation | async-start | bytes 4194304 | tf_op jit(solution)/shard_map/all_to_all | solution.py:212
  9.6 2.8 %fusion.15 = (f32[4,4,112,128]{3,2,1,0:T(8,128)}, f32[4,4,112,128]{3,2,1,0:T(8,128)}) fusion(f32[4,8,112,128]{3,2,1,0:T(8,128)} %param.5), kind=kLoop, calls=%fused_computation.48 | loop fusion | bytes 3670016 | tf_op jit(solution)/shard_map/slice | solution.py:24
  12.5 4.0 %collective-permute-start.2 = (f32[4,4,112,128]{3,2,1,0:T(8,128)}, f32[4,4,112,128]{3,2,1,0:T(8,128)}, u32[]{:S(2)}, u32[]{:S(2)}) collective-permute-start(f32[4,4,112,128]{3,2,1,0:T(8,128)} %get-tuple-element.46), channel_id=1, source_target_pairs={{0,1},{1,2},{2,3},{3,4},{4,5},{5,6},{6,7},{8,9},{9,10},{10,11},{11... | collective-permute-start | bytes 2752520 | tf_op jit(solution)/shard_map/ppermute | solution.py:23
  16.5 1.9 %collective-permute-start.3 = (f32[4,4,112,128]{3,2,1,0:T(8,128)}, f32[4,4,112,128]{3,2,1,0:T(8,128)}, u32[]{:S(2)}, u32[]{:S(2)}) collective-permute-start(f32[4,4,112,128]{3,2,1,0:T(8,128)} %get-tuple-element.45), channel_id=1, source_target_pairs={{1,0},{2,1},{3,2},{4,3},{5,4},{6,5},{7,6},{9,8},{10,9},{11,10},{12... | collective-permute-start | bytes 2752520 | tf_op jit(solution)/shard_map/ppermute | solution.py:24
  19.1 3.0 %pad_maximum_fusion.1 = f32[4,8,128,128]{3,2,1,0:T(8,128)} fusion(f32[1,8,128,128]{3,2,1,0:T(8,128)S(1)} %get-tuple-element.52, f32[1,8,128,128]{3,2,1,0:T(8,128)} %get-tuple-element.53, f32[1,8,128,128]{3,2,1,0:T(8,128)} %get-tuple-element.54, f32[1,8,128,128]{3,2,1,0:T(8,128)S(1)} %get-tuple-element.51), kind=kLoop, calls=%fused_computation.1 | loop fusion | flops 1572864 | bytes 4194304 | tf_op jit(solution)/shard_map/stack | solution.py:197
  22.2 4.9 %collective-permute-done.2 = f32[4,4,112,128]{3,2,1,0:T(8,128)} collective-permute-done((f32[4,4,112,128]{3,2,1,0:T(8,128)}, f32[4,4,112,128]{3,2,1,0:T(8,128)}, u32[]{:S(2)}, u32[]{:S(2)}) %collective-permute-start.2) | collective-permute-done | bytes 917536 | tf_op jit(solution)/shard_map/ppermute | solution.py:23
  27.1 1.2 constant_dynamic-update-slice_fusion.2
  28.5 3.2 %collective-permute-done.3 = f32[4,4,112,128]{3,2,1,0:T(8,128)} collective-permute-done((f32[4,4,112,128]{3,2,1,0:T(8,128)}, f32[4,4,112,128]{3,2,1,0:T(8,128)}, u32[]{:S(2)}, u32[]{:S(2)}) %collective-permute-start.3) | collective-permute-done | bytes 917536 | tf_op jit(solution)/shard_map/ppermute | solution.py:24
  31.7 1.2 constant_dynamic-update-slice_fusion
  33.0 3.7 %collective-permute-start.4 = (f32[4,16,8,128]{3,2,1,0:T(8,128)S(1)}, f32[4,16,8,128]{3,2,1,0:T(8,128)S(1)}, u32[]{:S(2)}, u32[]{:S(2)}) collective-permute-start(f32[4,16,8,128]{3,2,1,0:T(8,128)S(1)} %get-tuple-element.37), channel_id=1, source_target_pairs={{0,8},{8,16},{16,24},{1,9},{9,17},{17,25},{2,10},{10,18},{18,26},{... | collective-permute-start | bytes 786440 | tf_op jit(solution)/shard_map/ppermute | solution.py:23
  36.7 1.3 collective-permute-start.5
  38.0 4.5 %all-to-all-start.1 = ((f32[4,8,128,128]{3,2,1,0:T(8,128)}), f32[4,8,128,128]{3,2,1,0:T(8,128)}, u32[]{:S(2)}, u32[]{:S(2)}) async-start(f32[4,8,128,128]{3,2,1,0:T(8,128)} %pad_maximum_fusion.1), calls=%async_computation.1 | async-start | bytes 4194304 | tf_op jit(solution)/shard_map/all_to_all | solution.py:212
  42.7 2.4 %collective-permute-start = (f32[4,4,128,128]{3,2,1,0:T(8,128)S(1)}, f32[4,4,128,128]{3,2,1,0:T(8,128)S(1)}, u32[]{:S(2)}, u32[]{:S(2)}) collective-permute-start(f32[4,4,128,128]{3,2,1,0:T(8,128)S(1)} %get-tuple-element.44), channel_id=1, source_target_pairs={{0,1},{1,2},{2,3},{3,4},{4,5},{5,6},{6,7},{8,9},{9,10},{10,11},{11... | collective-permute-start | bytes 3145736 | tf_op jit(solution)/shard_map/ppermute | solution.py:23
  45.2 2.2 %collective-permute-start.1 = (f32[4,4,128,128]{3,2,1,0:T(8,128)S(1)}, f32[4,4,128,128]{3,2,1,0:T(8,128)S(1)}, u32[]{:S(2)}, u32[]{:S(2)}) collective-permute-start(f32[4,4,128,128]{3,2,1,0:T(8,128)S(1)} %get-tuple-element.43), channel_id=1, source_target_pairs={{1,0},{2,1},{3,2},{4,3},{5,4},{6,5},{7,6},{9,8},{10,9},{11,10},{12... | collective-permute-start | bytes 3145736 | tf_op jit(solution)/shard_map/ppermute | solution.py:24
  47.4 2.1 %collective-permute-done.5 = f32[4,16,8,128]{3,2,1,0:T(8,128)S(1)} collective-permute-done((f32[4,16,8,128]{3,2,1,0:T(8,128)S(1)}, f32[4,16,8,128]{3,2,1,0:T(8,128)S(1)}, u32[]{:S(2)}, u32[]{:S(2)}) %collective-permute-start.5) | collective-permute-done | bytes 262176 | tf_op jit(solution)/shard_map/ppermute | solution.py:24
  50.0 9.4 %shard_map.46.sums = f32[4,8,2,128,128]{4,3,2,1,0:T(8,128)S(1)} custom-call(f32[4,16,128,128]{3,2,1,0:T(8,128)S(1)} %pad_maximum_fusion.templates, bf16[128,384]{1,0:T(8,128)(2,1)S(1)} %add_convert_fusion.band_1, bf16[384,128]{1,0:T(8,128)(2,1)S(1)} %add_convert_fusion.1.band_y), custom_call_target="tpu_custom_call" | custom-call | flops 10000000000 | bytes 8388608 | tf_op jit(solution)/shard_map/pallas_call | solution.py:183
  59.4 2.1 %copy-done.1 = f32[4,8,2,128,128]{4,3,2,1,0:T(8,128)} copy-done((f32[4,8,2,128,128]{4,3,2,1,0:T(8,128)}, f32[4,8,2,128,128]{4,3,2,1,0:T(8,128)S(1)}, u32[]{:S(2)}) %copy-start.1) | copy-done | bytes 4194328
  61.7 18.1 %shard_map.47 = (f32[4,4,112,128]{3,2,1,0:T(8,128)S(1)}, f32[4,8,112,128]{3,2,1,0:T(8,128)S(1)}, f32[4,4,112,128]{3,2,1,0:T(8,128)S(1)}) custom-call(s32[2]{0:T(128)S(1)} %get-tuple-element.63.labels, s32[2]{0:T(128)S(1)} %get-tuple-element.56.live, f32[4,4,128,128]{3,2,1,0:T(8,128)S(1)} %collective-permute-done.low, f32[4,8,128,128]{3,2,1,0:T(8,128)} %copy-done.5, ...), custom_call_target="tpu_custom_call" | custom-call | flops 4000000000 | tf_op jit(solution)/shard_map/pallas_call | solution.py:225
  79.8 1.2 copy-done.2
  82.0 3.1 %fusion.13 = (f32[4,4,128,128]{3,2,1,0:T(8,128)}, f32[4,4,128,128]{3,2,1,0:T(8,128)}) fusion(f32[4,8,128,128]{3,2,1,0:T(8,128)} %all-to-all-done.1.mid), kind=kLoop, calls=%fused_computation.46 | loop fusion | bytes 4194304 | tf_op jit(solution)/shard_map/slice | solution.py:24
  85.1 2.0 %collective-permute-start.6 = (f32[4,4,128,128]{3,2,1,0:T(8,128)}, f32[4,4,128,128]{3,2,1,0:T(8,128)}, u32[]{:S(2)}, u32[]{:S(2)}) collective-permute-start(f32[4,4,128,128]{3,2,1,0:T(8,128)} %get-tuple-element.42), channel_id=1, source_target_pairs={{0,1},{1,2},{2,3},{3,4},{4,5},{5,6},{6,7},{8,9},{9,10},{10,11},{11... | collective-permute-start | bytes 3145736 | tf_op jit(solution)/shard_map/ppermute | solution.py:23
  87.1 3.3 %collective-permute-start.7 = (f32[4,4,128,128]{3,2,1,0:T(8,128)}, f32[4,4,128,128]{3,2,1,0:T(8,128)}, u32[]{:S(2)}, u32[]{:S(2)}) collective-permute-start(f32[4,4,128,128]{3,2,1,0:T(8,128)} %get-tuple-element.41), channel_id=1, source_target_pairs={{1,0},{2,1},{3,2},{4,3},{5,4},{6,5},{7,6},{9,8},{10,9},{11,10},{12... | collective-permute-start | bytes 3145736 | tf_op jit(solution)/shard_map/ppermute | solution.py:24
  91.7 19.8 %shard_map.48 = (f32[4,4,112,128]{3,2,1,0:T(8,128)S(1)}, f32[4,8,112,128]{3,2,1,0:T(8,128)}, f32[4,4,112,128]{3,2,1,0:T(8,128)S(1)}) custom-call(s32[2]{0:T(128)S(1)} %get-tuple-element.64.labels, s32[2]{0:T(128)S(1)} %get-tuple-element.55.live, f32[4,4,128,128]{3,2,1,0:T(8,128)S(1)} %collective-permute-done.low, f32[4,8,128,128]{3,2,1,0:T(8,128)} %copy-done.5, ...), custom_call_target="tpu_custom_call" | custom-call | flops 4000000000 | tf_op jit(solution)/shard_map/pallas_call | solution.py:225
  111.5 20.2 %shard_map.49 = (f32[4,4,112,128]{3,2,1,0:T(8,128)S(1)}, f32[4,8,112,128]{3,2,1,0:T(8,128)}, f32[4,4,112,128]{3,2,1,0:T(8,128)S(1)}) custom-call(s32[4]{0:T(128)S(1)} %slice.84.labels, s32[4]{0:T(128)S(1)} %slice.85.live, f32[4,4,128,128]{3,2,1,0:T(8,128)} %collective-permute-done.6.low, f32[4,8,128,128]{3,2,1,0:T(8,128)} %all-to-all-done.1.mid, ...), custom_call_target="tpu_custom_call" | custom-call | flops 8000000000 | tf_op jit(solution)/shard_map/pallas_call | solution.py:225
  131.7 2.9 %collective-permute-start.8 = (f32[4,4,112,128]{3,2,1,0:T(8,128)S(1)}, f32[4,4,112,128]{3,2,1,0:T(8,128)S(1)}, u32[]{:S(2)}, u32[]{:S(2)}) collective-permute-start(f32[4,4,112,128]{3,2,1,0:T(8,128)S(1)} %get-tuple-element.33), channel_id=1, source_target_pairs={{0,1},{1,2},{2,3},{3,4},{4,5},{5,6},{6,7},{8,9},{9,10},{10,11},{11... | collective-permute-start | bytes 2752520 | tf_op jit(solution)/shard_map/ppermute | solution.py:260
  134.6 1.9 %collective-permute-start.9 = (f32[4,4,112,128]{3,2,1,0:T(8,128)S(1)}, f32[4,4,112,128]{3,2,1,0:T(8,128)S(1)}, u32[]{:S(2)}, u32[]{:S(2)}) collective-permute-start(f32[4,4,112,128]{3,2,1,0:T(8,128)S(1)} %get-tuple-element.34), channel_id=1, source_target_pairs={{1,0},{2,1},{3,2},{4,3},{5,4},{6,5},{7,6},{9,8},{10,9},{11,10},{12... | collective-permute-start | bytes 2752520 | tf_op jit(solution)/shard_map/ppermute | solution.py:261
  136.6 8.3 %collective-permute-done.8 = f32[4,4,112,128]{3,2,1,0:T(8,128)S(1)} collective-permute-done((f32[4,4,112,128]{3,2,1,0:T(8,128)S(1)}, f32[4,4,112,128]{3,2,1,0:T(8,128)S(1)}, u32[]{:S(2)}, u32[]{:S(2)}) %collective-permute-start.8) | collective-permute-done | bytes 917536 | tf_op jit(solution)/shard_map/ppermute | solution.py:260
  144.9 4.4 %collective-permute-done.9 = f32[4,4,112,128]{3,2,1,0:T(8,128)S(1)} collective-permute-done((f32[4,4,112,128]{3,2,1,0:T(8,128)S(1)}, f32[4,4,112,128]{3,2,1,0:T(8,128)S(1)}, u32[]{:S(2)}, u32[]{:S(2)}) %collective-permute-start.9) | collective-permute-done | bytes 917536 | tf_op jit(solution)/shard_map/ppermute | solution.py:261
  149.3 3.2 %divide_add_fusion = f32[4,8,112,128]{3,2,1,0:T(8,128)} fusion(f32[4,8,112,128]{3,2,1,0:T(8,128)S(1)} %copy-done.7, f32[4,4,112,128]{3,2,1,0:T(8,128)S(1)} %collective-permute-done.9, f32[4,8,112,128]{3,2,1,0:T(8,128)} %get-tuple-element.32, f32[4,4,112,128]{3,2,1,0:T(8,128)S(1)} %collective-permute-done.8, f32[4]{0:T(128)S(1)} %convert_reduce_fusion), kind=kLoop, calls=%fused_computation.3 | loop fusion | flops 2293760 | bytes 7340048 | tf_op jit(solution)/shard_map/add | solution.py:266
  (51 shorter events, 4.3 us)
Async XLA Ops:
  5.4 32.6 %all-to-all-start = ((f32[4,8,128,128]{3,2,1,0:T(8,128)}), f32[4,8,128,128]{3,2,1,0:T(8,128)S(1)}, u32[]{:S(2)}, u32[]{:S(2)}) async-start(f32[4,8,128,128]{3,2,1,0:T(8,128)} %pad_maximum_fusion.2), calls=%async_computation | async-start | bytes 4194304 | tf_op jit(solution)/shard_map/all_to_all | solution.py:212
  9.6 8.9 %copy-start.10 = (s32[4]{0:T(128)S(1)}, s32[4]{0:T(128)}, u32[]{:S(2)}) copy-start(s32[4]{0:T(128)} %param.7) | copy-start | bytes 52
  9.6 9.4 %copy-start.11 = (s32[8]{0:T(128)S(1)}, s32[8]{0:T(128)}, u32[]{:S(2)}) copy-start(s32[8]{0:T(128)} %param.6) | copy-start | bytes 100
  12.5 14.7 %collective-permute-start.2 = (f32[4,4,112,128]{3,2,1,0:T(8,128)}, f32[4,4,112,128]{3,2,1,0:T(8,128)}, u32[]{:S(2)}, u32[]{:S(2)}) collective-permute-start(f32[4,4,112,128]{3,2,1,0:T(8,128)} %get-tuple-element.46), channel_id=1, source_target_pairs={{0,1},{1,2},{2,3},{3,4},{4,5},{5,6},{6,7},{8,9},{9,10},{10,11},{11... | collective-permute-start | bytes 2752520 | tf_op jit(solution)/shard_map/ppermute | solution.py:23
  16.5 15.2 %collective-permute-start.3 = (f32[4,4,112,128]{3,2,1,0:T(8,128)}, f32[4,4,112,128]{3,2,1,0:T(8,128)}, u32[]{:S(2)}, u32[]{:S(2)}) collective-permute-start(f32[4,4,112,128]{3,2,1,0:T(8,128)} %get-tuple-element.45), channel_id=1, source_target_pairs={{1,0},{2,1},{3,2},{4,3},{5,4},{6,5},{7,6},{9,8},{10,9},{11,10},{12... | collective-permute-start | bytes 2752520 | tf_op jit(solution)/shard_map/ppermute | solution.py:24
  19.1 9.3 %copy-start.6 = (f32[4,8,112,128]{3,2,1,0:T(8,128)S(1)}, f32[4,8,112,128]{3,2,1,0:T(8,128)}, u32[]{:S(2)}) copy-start(f32[4,8,112,128]{3,2,1,0:T(8,128)} %param.5) | copy-start | bytes 5505028
  33.0 3.7 %copy-start.8 = (f32[4,16,112,128]{3,2,1,0:T(8,128)}, f32[4,16,112,128]{3,2,1,0:T(8,128)S(1)}, u32[]{:S(2)}) copy-start(f32[4,16,112,128]{3,2,1,0:T(8,128)S(1)} %constant_dynamic-update-slice_fusion) | copy-start | bytes 11010052
  33.0 14.4 %collective-permute-start.4 = (f32[4,16,8,128]{3,2,1,0:T(8,128)S(1)}, f32[4,16,8,128]{3,2,1,0:T(8,128)S(1)}, u32[]{:S(2)}, u32[]{:S(2)}) collective-permute-start(f32[4,16,8,128]{3,2,1,0:T(8,128)S(1)} %get-tuple-element.37), channel_id=1, source_target_pairs={{0,8},{8,16},{16,24},{1,9},{9,17},{17,25},{2,10},{10,18},{18,26},{... | collective-permute-start | bytes 786440 | tf_op jit(solution)/shard_map/ppermute | solution.py:23
  36.7 12.8 %collective-permute-start.5 = (f32[4,16,8,128]{3,2,1,0:T(8,128)S(1)}, f32[4,16,8,128]{3,2,1,0:T(8,128)S(1)}, u32[]{:S(2)}, u32[]{:S(2)}) collective-permute-start(f32[4,16,8,128]{3,2,1,0:T(8,128)S(1)} %get-tuple-element.38), channel_id=1, source_target_pairs={{8,0},{16,8},{24,16},{9,1},{17,9},{25,17},{10,2},{18,10},{26,18},{... | collective-permute-start | bytes 786440 | tf_op jit(solution)/shard_map/ppermute | solution.py:24
  38.0 4.5 %copy-start.5 = (f32[4,8,128,128]{3,2,1,0:T(8,128)}, f32[4,8,128,128]{3,2,1,0:T(8,128)S(1)}, u32[]{:S(2)}) copy-start(f32[4,8,128,128]{3,2,1,0:T(8,128)S(1)} %all-to-all-done.mid) | copy-start | bytes 6291460
  38.0 43.9 %all-to-all-start.1 = ((f32[4,8,128,128]{3,2,1,0:T(8,128)}), f32[4,8,128,128]{3,2,1,0:T(8,128)}, u32[]{:S(2)}, u32[]{:S(2)}) async-start(f32[4,8,128,128]{3,2,1,0:T(8,128)} %pad_maximum_fusion.1), calls=%async_computation.1 | async-start | bytes 4194304 | tf_op jit(solution)/shard_map/all_to_all | solution.py:212
  42.5 7.0 %copy-start.9 = (f32[4,16,112,128]{3,2,1,0:T(8,128)S(1)}, f32[4,16,112,128]{3,2,1,0:T(8,128)}, u32[]{:S(2)}) copy-start(f32[4,16,112,128]{3,2,1,0:T(8,128)} %copy-done.8) | copy-start | bytes 11010052
  42.7 18.8 %collective-permute-start = (f32[4,4,128,128]{3,2,1,0:T(8,128)S(1)}, f32[4,4,128,128]{3,2,1,0:T(8,128)S(1)}, u32[]{:S(2)}, u32[]{:S(2)}) collective-permute-start(f32[4,4,128,128]{3,2,1,0:T(8,128)S(1)} %get-tuple-element.44), channel_id=1, source_target_pairs={{0,1},{1,2},{2,3},{3,4},{4,5},{5,6},{6,7},{8,9},{9,10},{10,11},{11... | collective-permute-start | bytes 3145736 | tf_op jit(solution)/shard_map/ppermute | solution.py:23
  45.2 16.5 %collective-permute-start.1 = (f32[4,4,128,128]{3,2,1,0:T(8,128)S(1)}, f32[4,4,128,128]{3,2,1,0:T(8,128)S(1)}, u32[]{:S(2)}, u32[]{:S(2)}) collective-permute-start(f32[4,4,128,128]{3,2,1,0:T(8,128)S(1)} %get-tuple-element.43), channel_id=1, source_target_pairs={{1,0},{2,1},{3,2},{4,3},{5,4},{6,5},{7,6},{9,8},{10,9},{11,10},{12... | collective-permute-start | bytes 3145736 | tf_op jit(solution)/shard_map/ppermute | solution.py:24
  50.0 9.4 %copy-start = (f32[4,16,128,128]{3,2,1,0:T(8,128)}, f32[4,16,128,128]{3,2,1,0:T(8,128)S(1)}, u32[]{:S(2)}) copy-start(f32[4,16,128,128]{3,2,1,0:T(8,128)S(1)} %pad_maximum_fusion.templates) | copy-start | bytes 12582916
  59.4 2.1 %copy-start.1 = (f32[4,8,2,128,128]{4,3,2,1,0:T(8,128)}, f32[4,8,2,128,128]{4,3,2,1,0:T(8,128)S(1)}, u32[]{:S(2)}) copy-start(f32[4,8,2,128,128]{4,3,2,1,0:T(8,128)S(1)} %shard_map.46.sums) | copy-start | bytes 12582916
  79.8 1.2 copy-start.2
  81.0 1.0 copy-start.3
  85.1 26.4 %collective-permute-start.6 = (f32[4,4,128,128]{3,2,1,0:T(8,128)}, f32[4,4,128,128]{3,2,1,0:T(8,128)}, u32[]{:S(2)}, u32[]{:S(2)}) collective-permute-start(f32[4,4,128,128]{3,2,1,0:T(8,128)} %get-tuple-element.42), channel_id=1, source_target_pairs={{0,1},{1,2},{2,3},{3,4},{4,5},{5,6},{6,7},{8,9},{9,10},{10,11},{11... | collective-permute-start | bytes 3145736 | tf_op jit(solution)/shard_map/ppermute | solution.py:23
  87.1 24.4 %collective-permute-start.7 = (f32[4,4,128,128]{3,2,1,0:T(8,128)}, f32[4,4,128,128]{3,2,1,0:T(8,128)}, u32[]{:S(2)}, u32[]{:S(2)}) collective-permute-start(f32[4,4,128,128]{3,2,1,0:T(8,128)} %get-tuple-element.41), channel_id=1, source_target_pairs={{1,0},{2,1},{3,2},{4,3},{5,4},{6,5},{7,6},{9,8},{10,9},{11,10},{12... | collective-permute-start | bytes 3145736 | tf_op jit(solution)/shard_map/ppermute | solution.py:24
  90.6 1.2 copy-start.4
  111.5 37.8 %copy-start.7 = (f32[4,8,112,128]{3,2,1,0:T(8,128)S(1)}, f32[4,8,112,128]{3,2,1,0:T(8,128)}, u32[]{:S(2)}) copy-start(f32[4,8,112,128]{3,2,1,0:T(8,128)} %param.5) | copy-start | bytes 5505028
  131.7 13.2 %collective-permute-start.8 = (f32[4,4,112,128]{3,2,1,0:T(8,128)S(1)}, f32[4,4,112,128]{3,2,1,0:T(8,128)S(1)}, u32[]{:S(2)}, u32[]{:S(2)}) collective-permute-start(f32[4,4,112,128]{3,2,1,0:T(8,128)S(1)} %get-tuple-element.33), channel_id=1, source_target_pairs={{0,1},{1,2},{2,3},{3,4},{4,5},{5,6},{6,7},{8,9},{9,10},{10,11},{11... | collective-permute-start | bytes 2752520 | tf_op jit(solution)/shard_map/ppermute | solution.py:260
  134.6 14.7 %collective-permute-start.9 = (f32[4,4,112,128]{3,2,1,0:T(8,128)S(1)}, f32[4,4,112,128]{3,2,1,0:T(8,128)S(1)}, u32[]{:S(2)}, u32[]{:S(2)}) collective-permute-start(f32[4,4,112,128]{3,2,1,0:T(8,128)S(1)} %get-tuple-element.34), channel_id=1, source_target_pairs={{1,0},{2,1},{3,2},{4,3},{5,4},{6,5},{7,6},{9,8},{10,9},{11,10},{12... | collective-permute-start | bytes 2752520 | tf_op jit(solution)/shard_map/ppermute | solution.py:261

commit v3 on v2

--- a/solution.py
+++ b/solution.py
@@ -36,8 +36,10 @@
 def plane_box(planes, band_x, band_y):
     count = len(planes)
     rows = band_x.shape[0]
+    width = planes[0].shape[1]
     terms = [jnp.concatenate(thirds(plane), axis=0) for plane in planes]
-    along_x = [jnp.dot(band_x, term, preferred_element_type=jnp.float32) for term in terms]
+    wide = jnp.dot(band_x, jnp.concatenate(terms, axis=1), preferred_element_type=jnp.float32)
+    along_x = [wide[:, i * width : (i + 1) * width] for i in range(count)]
     stacked = jnp.concatenate([jnp.concatenate(thirds(v), axis=1) for v in along_x], axis=0)
     summed = jnp.dot(stacked, band_y, preferred_element_type=jnp.float32)
     return [summed[i * rows : (i + 1) * rows] for i in range(count)]
@@ -104,7 +106,7 @@
                 boxes[z, channel] = result[channel]
             return carry
 
-        lax.fori_loop(0, depth, layer, 0, unroll=2)
+        lax.fori_loop(0, depth, layer, 0, unroll=4)
 
         chunk = 16 if own % 16 == 0 else 8
 

time: 151 us -> 149 us (0.987); the launches traced: 153 us -> 147 us
  Pallas kernels: 67.4 us -> 61.9 us
    pallas_call x3, Pallas kernels: 58 us -> 53.3 us  [per_device(): pl.pallas_call(kernel, grid_spec=pltpu.PrefetchScalarGridSpec(num_scalar_...]
  transfers between devices with their start and end apart: 12 -> 12, of which waited for: 6 -> 6; matrix products, arithmetic and copies ran while one was open for 7% -> 7% of each run, Pallas kernels for 31% -> 29%
where the time goes in v3:
time: 149 us; the launch traced here: 147 us
  Pallas kernels  61.9 us (42%)
  starting transfers between devices  33.9 us (23%)
  waiting for transfers between devices  23.6 us (16%)
  local copies, waits for them, and re-layouts  18.7 us (13%)
  other arithmetic  8.64 us (6%)
    pallas_call x3, Pallas kernels, per_device(): pl.pallas_call(kernel, grid_spec=pltpu.PrefetchScalarGridSpec(num_scalar_...  53.3 us
    ppermute x4, starting transfers between devices, halo(): lax.ppermute(lax.slice_in_dim(block, size - width, size, axis=dim), axis,...  12 us
    ppermute x4, starting transfers between devices, halo(): lax.ppermute(lax.slice_in_dim(block, 0, width, axis=dim), axis, backward)  8.79 us
    all_to_all x2, starting transfers between devices, per_device(): arrived.append(lax.all_to_all(send, 'subj', 0, 0, tiled=True))  8.72 us
    pallas_call x1, Pallas kernels, per_device(): pl.pallas_call(template_kernel, grid=(clusters,), in_specs=[step_block(t_...  8.54 us
    ppermute x1, waiting for transfers between devices, per_device(): from_low = lax.ppermute(totals[2], 'slab', forward)  8.01 us
    unnamed x26, local copies, waits for them, and re-layouts  6.85 us
    ppermute x4, waiting for transfers between devices, halo(): lax.ppermute(lax.slice_in_dim(block, 0, width, axis=dim), axis, backward)  6.32 us
  transfers between devices with their start and end apart: 12, of which 6 were waited for; matrix products, arithmetic and copies ran while one was open for 7% of the time, Pallas kernels for 29%

profile of v3, /device:TPU:1, one launch (start us, length us, event | category | flops | bytes accessed | tf_op | source)
XLA Modules:
  0.0 147.2 jit_solution(13799771837411529364)
XLA Ops:
  0.0 2.3 %slice_bitcast_fusion = (f32[8,448,128]{2,1,0:T(8,128)S(1)}, f32[8,448,128]{2,1,0:T(8,128)S(1)}) fusion(f32[2,8,448,128]{3,2,1,0:T(8,128)} %param.4), kind=kLoop, calls=%fused_computation.4 | loop fusion | bytes 7340032 | tf_op jit(solution)/shard_map/squeeze | solution.py:198
  2.3 1.5 %fusion = (f32[1,8,128,128]{3,2,1,0:T(8,128)S(1)}, f32[1,8,128,128]{3,2,1,0:T(8,128)S(1)}, f32[1,8,128,128]{3,2,1,0:T(8,128)}, f32[1,8,128,128]{3,2,1,0:T(8,128)...) fusion(f32[8,448,128]{2,1,0:T(8,128)S(1)} %get-tuple-element.40, ...), kind=kLoop, calls=%fused_computation.10 | loop fusion | bytes 9961472 | tf_op jit(solution)/shard_map/stack | solution.py:199
  3.9 1.5 %pad_maximum_fusion.2 = f32[4,8,128,128]{3,2,1,0:T(8,128)} fusion(f32[1,8,128,128]{3,2,1,0:T(8,128)S(1)} %get-tuple-element.61, f32[1,8,128,128]{3,2,1,0:T(8,128)S(1)} %get-tuple-element.60, f32[1,8,128,128]{3,2,1,0:T(8,128)S(1)} %get-tuple-element.59, f32[1,8,128,128]{3,2,1,0:T(8,128)S(1)} %get-tuple-element.62), kind=kLoop, calls=%fused_computation.2 | loop fusion | flops 1572864 | bytes 4194304 | tf_op jit(solution)/shard_map/stack | solution.py:199
  5.4 4.3 %all-to-all-start = ((f32[4,8,128,128]{3,2,1,0:T(8,128)}), f32[4,8,128,128]{3,2,1,0:T(8,128)S(1)}, u32[]{:S(2)}, u32[]{:S(2)}) async-start(f32[4,8,128,128]{3,2,1,0:T(8,128)} %pad_maximum_fusion.2), calls=%async_computation | async-start | bytes 4194304 | tf_op jit(solution)/shard_map/all_to_all | solution.py:214
  9.6 2.8 %fusion.15 = (f32[4,4,112,128]{3,2,1,0:T(8,128)}, f32[4,4,112,128]{3,2,1,0:T(8,128)}) fusion(f32[4,8,112,128]{3,2,1,0:T(8,128)} %param.5), kind=kLoop, calls=%fused_computation.48 | loop fusion | bytes 3670016 | tf_op jit(solution)/shard_map/slice | solution.py:24
  12.5 4.0 %collective-permute-start.2 = (f32[4,4,112,128]{3,2,1,0:T(8,128)}, f32[4,4,112,128]{3,2,1,0:T(8,128)}, u32[]{:S(2)}, u32[]{:S(2)}) collective-permute-start(f32[4,4,112,128]{3,2,1,0:T(8,128)} %get-tuple-element.46), channel_id=1, source_target_pairs={{0,1},{1,2},{2,3},{3,4},{4,5},{5,6},{6,7},{8,9},{9,10},{10,11},{11... | collective-permute-start | bytes 2752520 | tf_op jit(solution)/shard_map/ppermute | solution.py:23
  16.5 1.9 %collective-permute-start.3 = (f32[4,4,112,128]{3,2,1,0:T(8,128)}, f32[4,4,112,128]{3,2,1,0:T(8,128)}, u32[]{:S(2)}, u32[]{:S(2)}) collective-permute-start(f32[4,4,112,128]{3,2,1,0:T(8,128)} %get-tuple-element.45), channel_id=1, source_target_pairs={{1,0},{2,1},{3,2},{4,3},{5,4},{6,5},{7,6},{9,8},{10,9},{11,10},{12... | collective-permute-start | bytes 2752520 | tf_op jit(solution)/shard_map/ppermute | solution.py:24
  19.1 3.0 %pad_maximum_fusion.1 = f32[4,8,128,128]{3,2,1,0:T(8,128)} fusion(f32[1,8,128,128]{3,2,1,0:T(8,128)S(1)} %get-tuple-element.52, f32[1,8,128,128]{3,2,1,0:T(8,128)} %get-tuple-element.53, f32[1,8,128,128]{3,2,1,0:T(8,128)} %get-tuple-element.54, f32[1,8,128,128]{3,2,1,0:T(8,128)S(1)} %get-tuple-element.51), kind=kLoop, calls=%fused_computation.1 | loop fusion | flops 1572864 | bytes 4194304 | tf_op jit(solution)/shard_map/stack | solution.py:199
  22.2 4.9 %collective-permute-done.2 = f32[4,4,112,128]{3,2,1,0:T(8,128)} collective-permute-done((f32[4,4,112,128]{3,2,1,0:T(8,128)}, f32[4,4,112,128]{3,2,1,0:T(8,128)}, u32[]{:S(2)}, u32[]{:S(2)}) %collective-permute-start.2) | collective-permute-done | bytes 917536 | tf_op jit(solution)/shard_map/ppermute | solution.py:23
  27.1 1.2 constant_dynamic-update-slice_fusion.2
  28.5 3.2 %collective-permute-done.3 = f32[4,4,112,128]{3,2,1,0:T(8,128)} collective-permute-done((f32[4,4,112,128]{3,2,1,0:T(8,128)}, f32[4,4,112,128]{3,2,1,0:T(8,128)}, u32[]{:S(2)}, u32[]{:S(2)}) %collective-permute-start.3) | collective-permute-done | bytes 917536 | tf_op jit(solution)/shard_map/ppermute | solution.py:24
  31.7 1.2 constant_dynamic-update-slice_fusion
  33.0 3.7 %collective-permute-start.4 = (f32[4,16,8,128]{3,2,1,0:T(8,128)S(1)}, f32[4,16,8,128]{3,2,1,0:T(8,128)S(1)}, u32[]{:S(2)}, u32[]{:S(2)}) collective-permute-start(f32[4,16,8,128]{3,2,1,0:T(8,128)S(1)} %get-tuple-element.37), channel_id=1, source_target_pairs={{0,8},{8,16},{16,24},{1,9},{9,17},{17,25},{2,10},{10,18},{18,26},{... | collective-permute-start | bytes 786440 | tf_op jit(solution)/shard_map/ppermute | solution.py:23
  36.7 1.3 collective-permute-start.5
  38.0 4.5 %all-to-all-start.1 = ((f32[4,8,128,128]{3,2,1,0:T(8,128)}), f32[4,8,128,128]{3,2,1,0:T(8,128)}, u32[]{:S(2)}, u32[]{:S(2)}) async-start(f32[4,8,128,128]{3,2,1,0:T(8,128)} %pad_maximum_fusion.1), calls=%async_computation.1 | async-start | bytes 4194304 | tf_op jit(solution)/shard_map/all_to_all | solution.py:214
  42.7 2.4 %collective-permute-start = (f32[4,4,128,128]{3,2,1,0:T(8,128)S(1)}, f32[4,4,128,128]{3,2,1,0:T(8,128)S(1)}, u32[]{:S(2)}, u32[]{:S(2)}) collective-permute-start(f32[4,4,128,128]{3,2,1,0:T(8,128)S(1)} %get-tuple-element.44), channel_id=1, source_target_pairs={{0,1},{1,2},{2,3},{3,4},{4,5},{5,6},{6,7},{8,9},{9,10},{10,11},{11... | collective-permute-start | bytes 3145736 | tf_op jit(solution)/shard_map/ppermute | solution.py:23
  45.2 2.2 %collective-permute-start.1 = (f32[4,4,128,128]{3,2,1,0:T(8,128)S(1)}, f32[4,4,128,128]{3,2,1,0:T(8,128)S(1)}, u32[]{:S(2)}, u32[]{:S(2)}) collective-permute-start(f32[4,4,128,128]{3,2,1,0:T(8,128)S(1)} %get-tuple-element.43), channel_id=1, source_target_pairs={{1,0},{2,1},{3,2},{4,3},{5,4},{6,5},{7,6},{9,8},{10,9},{11,10},{12... | collective-permute-start | bytes 3145736 | tf_op jit(solution)/shard_map/ppermute | solution.py:24
  47.4 2.1 %collective-permute-done.5 = f32[4,16,8,128]{3,2,1,0:T(8,128)S(1)} collective-permute-done((f32[4,16,8,128]{3,2,1,0:T(8,128)S(1)}, f32[4,16,8,128]{3,2,1,0:T(8,128)S(1)}, u32[]{:S(2)}, u32[]{:S(2)}) %collective-permute-start.5) | collective-permute-done | bytes 262176 | tf_op jit(solution)/shard_map/ppermute | solution.py:24
  50.0 8.5 %shard_map.46.sums = f32[4,8,2,128,128]{4,3,2,1,0:T(8,128)S(1)} custom-call(f32[4,16,128,128]{3,2,1,0:T(8,128)S(1)} %pad_maximum_fusion.templates, bf16[128,384]{1,0:T(8,128)(2,1)S(1)} %add_convert_fusion.band_1, bf16[384,128]{1,0:T(8,128)(2,1)S(1)} %add_convert_fusion.1.band_y), custom_call_target="tpu_custom_call" | custom-call | flops 10000000000 | bytes 8388608 | tf_op jit(solution)/shard_map/pallas_call | solution.py:185
  58.6 2.1 %copy-done.1 = f32[4,8,2,128,128]{4,3,2,1,0:T(8,128)} copy-done((f32[4,8,2,128,128]{4,3,2,1,0:T(8,128)}, f32[4,8,2,128,128]{4,3,2,1,0:T(8,128)S(1)}, u32[]{:S(2)}) %copy-start.1) | copy-done | bytes 4194328
  61.7 16.1 %shard_map.47 = (f32[4,4,112,128]{3,2,1,0:T(8,128)S(1)}, f32[4,8,112,128]{3,2,1,0:T(8,128)S(1)}, f32[4,4,112,128]{3,2,1,0:T(8,128)S(1)}) custom-call(s32[2]{0:T(128)S(1)} %get-tuple-element.63.labels, s32[2]{0:T(128)S(1)} %get-tuple-element.56.live, f32[4,4,128,128]{3,2,1,0:T(8,128)S(1)} %collective-permute-done.low, f32[4,8,128,128]{3,2,1,0:T(8,128)} %copy-done.5, ...), custom_call_target="tpu_custom_call" | custom-call | flops 4000000000 | tf_op jit(solution)/shard_map/pallas_call | solution.py:227
  77.9 1.2 copy-done.2
  80.1 3.1 %fusion.13 = (f32[4,4,128,128]{3,2,1,0:T(8,128)}, f32[4,4,128,128]{3,2,1,0:T(8,128)}) fusion(f32[4,8,128,128]{3,2,1,0:T(8,128)} %all-to-all-done.1.mid), kind=kLoop, calls=%fused_computation.46 | loop fusion | bytes 4194304 | tf_op jit(solution)/shard_map/slice | solution.py:24
  83.2 1.9 %collective-permute-start.6 = (f32[4,4,128,128]{3,2,1,0:T(8,128)}, f32[4,4,128,128]{3,2,1,0:T(8,128)}, u32[]{:S(2)}, u32[]{:S(2)}) collective-permute-start(f32[4,4,128,128]{3,2,1,0:T(8,128)} %get-tuple-element.42), channel_id=1, source_target_pairs={{0,1},{1,2},{2,3},{3,4},{4,5},{5,6},{6,7},{8,9},{9,10},{10,11},{11... | collective-permute-start | bytes 3145736 | tf_op jit(solution)/shard_map/ppermute | solution.py:23
  85.1 3.4 %collective-permute-start.7 = (f32[4,4,128,128]{3,2,1,0:T(8,128)}, f32[4,4,128,128]{3,2,1,0:T(8,128)}, u32[]{:S(2)}, u32[]{:S(2)}) collective-permute-start(f32[4,4,128,128]{3,2,1,0:T(8,128)} %get-tuple-element.41), channel_id=1, source_target_pairs={{1,0},{2,1},{3,2},{4,3},{5,4},{6,5},{7,6},{9,8},{10,9},{11,10},{12... | collective-permute-start | bytes 3145736 | tf_op jit(solution)/shard_map/ppermute | solution.py:24
  89.8 17.8 %shard_map.48 = (f32[4,4,112,128]{3,2,1,0:T(8,128)S(1)}, f32[4,8,112,128]{3,2,1,0:T(8,128)}, f32[4,4,112,128]{3,2,1,0:T(8,128)S(1)}) custom-call(s32[2]{0:T(128)S(1)} %get-tuple-element.64.labels, s32[2]{0:T(128)S(1)} %get-tuple-element.55.live, f32[4,4,128,128]{3,2,1,0:T(8,128)S(1)} %collective-permute-done.low, f32[4,8,128,128]{3,2,1,0:T(8,128)} %copy-done.5, ...), custom_call_target="tpu_custom_call" | custom-call | flops 4000000000 | tf_op jit(solution)/shard_map/pallas_call | solution.py:227
  107.7 19.4 %shard_map.49 = (f32[4,4,112,128]{3,2,1,0:T(8,128)S(1)}, f32[4,8,112,128]{3,2,1,0:T(8,128)}, f32[4,4,112,128]{3,2,1,0:T(8,128)S(1)}) custom-call(s32[4]{0:T(128)S(1)} %slice.84.labels, s32[4]{0:T(128)S(1)} %slice.85.live, f32[4,4,128,128]{3,2,1,0:T(8,128)} %collective-permute-done.6.low, f32[4,8,128,128]{3,2,1,0:T(8,128)} %all-to-all-done.1.mid, ...), custom_call_target="tpu_custom_call" | custom-call | flops 8000000000 | tf_op jit(solution)/shard_map/pallas_call | solution.py:227
  127.0 2.2 %collective-permute-start.8 = (f32[4,4,112,128]{3,2,1,0:T(8,128)S(1)}, f32[4,4,112,128]{3,2,1,0:T(8,128)S(1)}, u32[]{:S(2)}, u32[]{:S(2)}) collective-permute-start(f32[4,4,112,128]{3,2,1,0:T(8,128)S(1)} %get-tuple-element.33), channel_id=1, source_target_pairs={{0,1},{1,2},{2,3},{3,4},{4,5},{5,6},{6,7},{8,9},{9,10},{10,11},{11... | collective-permute-start | bytes 2752520 | tf_op jit(solution)/shard_map/ppermute | solution.py:262
  129.2 2.2 %collective-permute-start.9 = (f32[4,4,112,128]{3,2,1,0:T(8,128)S(1)}, f32[4,4,112,128]{3,2,1,0:T(8,128)S(1)}, u32[]{:S(2)}, u32[]{:S(2)}) collective-permute-start(f32[4,4,112,128]{3,2,1,0:T(8,128)S(1)} %get-tuple-element.34), channel_id=1, source_target_pairs={{1,0},{2,1},{3,2},{4,3},{5,4},{6,5},{7,6},{9,8},{10,9},{11,10},{12... | collective-permute-start | bytes 2752520 | tf_op jit(solution)/shard_map/ppermute | solution.py:263
  131.6 8.0 %collective-permute-done.8 = f32[4,4,112,128]{3,2,1,0:T(8,128)S(1)} collective-permute-done((f32[4,4,112,128]{3,2,1,0:T(8,128)S(1)}, f32[4,4,112,128]{3,2,1,0:T(8,128)S(1)}, u32[]{:S(2)}, u32[]{:S(2)}) %collective-permute-start.8) | collective-permute-done | bytes 917536 | tf_op jit(solution)/shard_map/ppermute | solution.py:262
  139.6 4.4 %collective-permute-done.9 = f32[4,4,112,128]{3,2,1,0:T(8,128)S(1)} collective-permute-done((f32[4,4,112,128]{3,2,1,0:T(8,128)S(1)}, f32[4,4,112,128]{3,2,1,0:T(8,128)S(1)}, u32[]{:S(2)}, u32[]{:S(2)}) %collective-permute-start.9) | collective-permute-done | bytes 917536 | tf_op jit(solution)/shard_map/ppermute | solution.py:263
  144.0 3.2 %divide_add_fusion = f32[4,8,112,128]{3,2,1,0:T(8,128)} fusion(f32[4,8,112,128]{3,2,1,0:T(8,128)S(1)} %copy-done.7, f32[4,4,112,128]{3,2,1,0:T(8,128)S(1)} %collective-permute-done.9, f32[4,8,112,128]{3,2,1,0:T(8,128)} %get-tuple-element.32, f32[4,4,112,128]{3,2,1,0:T(8,128)S(1)} %collective-permute-done.8, f32[4]{0:T(128)S(1)} %convert_reduce_fusion), kind=kLoop, calls=%fused_computation.3 | loop fusion | flops 2293760 | bytes 7340048 | tf_op jit(solution)/shard_map/add | solution.py:268
  (51 shorter events, 5.2 us)
Async XLA Ops:
  5.4 32.6 %all-to-all-start = ((f32[4,8,128,128]{3,2,1,0:T(8,128)}), f32[4,8,128,128]{3,2,1,0:T(8,128)S(1)}, u32[]{:S(2)}, u32[]{:S(2)}) async-start(f32[4,8,128,128]{3,2,1,0:T(8,128)} %pad_maximum_fusion.2), calls=%async_computation | async-start | bytes 4194304 | tf_op jit(solution)/shard_map/all_to_all | solution.py:214
  9.6 8.9 %copy-start.10 = (s32[4]{0:T(128)S(1)}, s32[4]{0:T(128)}, u32[]{:S(2)}) copy-start(s32[4]{0:T(128)} %param.7) | copy-start | bytes 52
  9.6 9.4 %copy-start.11 = (s32[8]{0:T(128)S(1)}, s32[8]{0:T(128)}, u32[]{:S(2)}) copy-start(s32[8]{0:T(128)} %param.6) | copy-start | bytes 100
  12.5 14.7 %collective-permute-start.2 = (f32[4,4,112,128]{3,2,1,0:T(8,128)}, f32[4,4,112,128]{3,2,1,0:T(8,128)}, u32[]{:S(2)}, u32[]{:S(2)}) collective-permute-start(f32[4,4,112,128]{3,2,1,0:T(8,128)} %get-tuple-element.46), channel_id=1, source_target_pairs={{0,1},{1,2},{2,3},{3,4},{4,5},{5,6},{6,7},{8,9},{9,10},{10,11},{11... | collective-permute-start | bytes 2752520 | tf_op jit(solution)/shard_map/ppermute | solution.py:23
  16.5 15.2 %collective-permute-start.3 = (f32[4,4,112,128]{3,2,1,0:T(8,128)}, f32[4,4,112,128]{3,2,1,0:T(8,128)}, u32[]{:S(2)}, u32[]{:S(2)}) collective-permute-start(f32[4,4,112,128]{3,2,1,0:T(8,128)} %get-tuple-element.45), channel_id=1, source_target_pairs={{1,0},{2,1},{3,2},{4,3},{5,4},{6,5},{7,6},{9,8},{10,9},{11,10},{12... | collective-permute-start | bytes 2752520 | tf_op jit(solution)/shard_map/ppermute | solution.py:24
  19.1 9.3 %copy-start.6 = (f32[4,8,112,128]{3,2,1,0:T(8,128)S(1)}, f32[4,8,112,128]{3,2,1,0:T(8,128)}, u32[]{:S(2)}) copy-start(f32[4,8,112,128]{3,2,1,0:T(8,128)} %param.5) | copy-start | bytes 5505028
  33.0 3.7 %copy-start.8 = (f32[4,16,112,128]{3,2,1,0:T(8,128)}, f32[4,16,112,128]{3,2,1,0:T(8,128)S(1)}, u32[]{:S(2)}) copy-start(f32[4,16,112,128]{3,2,1,0:T(8,128)S(1)} %constant_dynamic-update-slice_fusion) | copy-start | bytes 11010052
  33.0 14.4 %collective-permute-start.4 = (f32[4,16,8,128]{3,2,1,0:T(8,128)S(1)}, f32[4,16,8,128]{3,2,1,0:T(8,128)S(1)}, u32[]{:S(2)}, u32[]{:S(2)}) collective-permute-start(f32[4,16,8,128]{3,2,1,0:T(8,128)S(1)} %get-tuple-element.37), channel_id=1, source_target_pairs={{0,8},{8,16},{16,24},{1,9},{9,17},{17,25},{2,10},{10,18},{18,26},{... | collective-permute-start | bytes 786440 | tf_op jit(solution)/shard_map/ppermute | solution.py:23
  36.7 12.8 %collective-permute-start.5 = (f32[4,16,8,128]{3,2,1,0:T(8,128)S(1)}, f32[4,16,8,128]{3,2,1,0:T(8,128)S(1)}, u32[]{:S(2)}, u32[]{:S(2)}) collective-permute-start(f32[4,16,8,128]{3,2,1,0:T(8,128)S(1)} %get-tuple-element.38), channel_id=1, source_target_pairs={{8,0},{16,8},{24,16},{9,1},{17,9},{25,17},{10,2},{18,10},{26,18},{... | collective-permute-start | bytes 786440 | tf_op jit(solution)/shard_map/ppermute | solution.py:24
  38.0 4.5 %copy-start.5 = (f32[4,8,128,128]{3,2,1,0:T(8,128)}, f32[4,8,128,128]{3,2,1,0:T(8,128)S(1)}, u32[]{:S(2)}) copy-start(f32[4,8,128,128]{3,2,1,0:T(8,128)S(1)} %all-to-all-done.mid) | copy-start | bytes 6291460
  38.0 42.0 %all-to-all-start.1 = ((f32[4,8,128,128]{3,2,1,0:T(8,128)}), f32[4,8,128,128]{3,2,1,0:T(8,128)}, u32[]{:S(2)}, u32[]{:S(2)}) async-start(f32[4,8,128,128]{3,2,1,0:T(8,128)} %pad_maximum_fusion.1), calls=%async_computation.1 | async-start | bytes 4194304 | tf_op jit(solution)/shard_map/all_to_all | solution.py:214
  42.5 7.0 %copy-start.9 = (f32[4,16,112,128]{3,2,1,0:T(8,128)S(1)}, f32[4,16,112,128]{3,2,1,0:T(8,128)}, u32[]{:S(2)}) copy-start(f32[4,16,112,128]{3,2,1,0:T(8,128)} %copy-done.8) | copy-start | bytes 11010052
  42.7 17.9 %collective-permute-start = (f32[4,4,128,128]{3,2,1,0:T(8,128)S(1)}, f32[4,4,128,128]{3,2,1,0:T(8,128)S(1)}, u32[]{:S(2)}, u32[]{:S(2)}) collective-permute-start(f32[4,4,128,128]{3,2,1,0:T(8,128)S(1)} %get-tuple-element.44), channel_id=1, source_target_pairs={{0,1},{1,2},{2,3},{3,4},{4,5},{5,6},{6,7},{8,9},{9,10},{10,11},{11... | collective-permute-start | bytes 3145736 | tf_op jit(solution)/shard_map/ppermute | solution.py:23
  45.2 16.5 %collective-permute-start.1 = (f32[4,4,128,128]{3,2,1,0:T(8,128)S(1)}, f32[4,4,128,128]{3,2,1,0:T(8,128)S(1)}, u32[]{:S(2)}, u32[]{:S(2)}) collective-permute-start(f32[4,4,128,128]{3,2,1,0:T(8,128)S(1)} %get-tuple-element.43), channel_id=1, source_target_pairs={{1,0},{2,1},{3,2},{4,3},{5,4},{6,5},{7,6},{9,8},{10,9},{11,10},{12... | collective-permute-start | bytes 3145736 | tf_op jit(solution)/shard_map/ppermute | solution.py:24
  50.0 8.6 %copy-start = (f32[4,16,128,128]{3,2,1,0:T(8,128)}, f32[4,16,128,128]{3,2,1,0:T(8,128)S(1)}, u32[]{:S(2)}) copy-start(f32[4,16,128,128]{3,2,1,0:T(8,128)S(1)} %pad_maximum_fusion.templates) | copy-start | bytes 12582916
  58.6 2.1 %copy-start.1 = (f32[4,8,2,128,128]{4,3,2,1,0:T(8,128)}, f32[4,8,2,128,128]{4,3,2,1,0:T(8,128)S(1)}, u32[]{:S(2)}) copy-start(f32[4,8,2,128,128]{4,3,2,1,0:T(8,128)S(1)} %shard_map.46.sums) | copy-start | bytes 12582916
  77.9 1.2 copy-start.2
  79.1 1.0 copy-start.3
  83.2 24.5 %collective-permute-start.6 = (f32[4,4,128,128]{3,2,1,0:T(8,128)}, f32[4,4,128,128]{3,2,1,0:T(8,128)}, u32[]{:S(2)}, u32[]{:S(2)}) collective-permute-start(f32[4,4,128,128]{3,2,1,0:T(8,128)} %get-tuple-element.42), channel_id=1, source_target_pairs={{0,1},{1,2},{2,3},{3,4},{4,5},{5,6},{6,7},{8,9},{9,10},{10,11},{11... | collective-permute-start | bytes 3145736 | tf_op jit(solution)/shard_map/ppermute | solution.py:23
  85.1 22.6 %collective-permute-start.7 = (f32[4,4,128,128]{3,2,1,0:T(8,128)}, f32[4,4,128,128]{3,2,1,0:T(8,128)}, u32[]{:S(2)}, u32[]{:S(2)}) collective-permute-start(f32[4,4,128,128]{3,2,1,0:T(8,128)} %get-tuple-element.41), channel_id=1, source_target_pairs={{1,0},{2,1},{3,2},{4,3},{5,4},{6,5},{7,6},{9,8},{10,9},{11,10},{12... | collective-permute-start | bytes 3145736 | tf_op jit(solution)/shard_map/ppermute | solution.py:24
  88.6 1.2 copy-start.4
  107.7 36.3 %copy-start.7 = (f32[4,8,112,128]{3,2,1,0:T(8,128)S(1)}, f32[4,8,112,128]{3,2,1,0:T(8,128)}, u32[]{:S(2)}) copy-start(f32[4,8,112,128]{3,2,1,0:T(8,128)} %param.5) | copy-start | bytes 5505028
  127.0 12.5 %collective-permute-start.8 = (f32[4,4,112,128]{3,2,1,0:T(8,128)S(1)}, f32[4,4,112,128]{3,2,1,0:T(8,128)S(1)}, u32[]{:S(2)}, u32[]{:S(2)}) collective-permute-start(f32[4,4,112,128]{3,2,1,0:T(8,128)S(1)} %get-tuple-element.33), channel_id=1, source_target_pairs={{0,1},{1,2},{2,3},{3,4},{4,5},{5,6},{6,7},{8,9},{9,10},{10,11},{11... | collective-permute-start | bytes 2752520 | tf_op jit(solution)/shard_map/ppermute | solution.py:262
  129.2 14.7 %collective-permute-start.9 = (f32[4,4,112,128]{3,2,1,0:T(8,128)S(1)}, f32[4,4,112,128]{3,2,1,0:T(8,128)S(1)}, u32[]{:S(2)}, u32[]{:S(2)}) collective-permute-start(f32[4,4,112,128]{3,2,1,0:T(8,128)S(1)} %get-tuple-element.34), channel_id=1, source_target_pairs={{1,0},{2,1},{3,2},{4,3},{5,4},{6,5},{7,6},{9,8},{10,9},{11,10},{12... | collective-permute-start | bytes 2752520 | tf_op jit(solution)/shard_map/ppermute | solution.py:263
